TPU v7x, 256 devices: a whole 4x4x8 slice. The times are simulated.
256 devices in a mesh: section: 4 (over x_hi, core), dp: 64 (over z, y, x_lo).
Axes of the slice: x: 4 (x_hi: 2, x_lo: 2; x = x_hi * 2 + x_lo), y: 4, z: 8, core: 2. Of those that a mesh axis runs over, the one named last changes fastest.
Arguments:
- top_grad: bfloat16 [16384, 3584], P('dp'), may hold values from -6 to 6
- activations: bfloat16 [4, 16384, 3584], P('section', 'dp'), may hold values from -6 to 6
- weights: bfloat16 [4, 3584, 3584], P('section', 'dp'), may hold values from -0.09375 to 0.09375
- proj_in: bfloat16 [4, 64, 3584], P('section'), may hold values from -0.09375 to 0.09375
- proj_out: bfloat16 [4, 64, 3584], P('section'), may hold values from -0.09375 to 0.09375
- queries: bfloat16 [4, 128, 4096], P('section', 'dp'), may hold values from -6 to 6
- lengths: int32 [128], P('dp'), may hold values from 32 to 128
Outputs:
- scores: float32 [128, 128], P('dp', 'section')
All inputs are finite; a program needn't handle non-finite values.
Results may differ from a plain program's by a relative error of at most 0.013.
Values may be sent and summed in bfloat16 or wider, within the bound.
A program may use at most 128 MiB of HBM per device.

v0:
```python
import jax
import jax.numpy as jnp
from jax import lax
from jax.sharding import PartitionSpec as P


def passed_along(value, axis, steps):
    count = lax.axis_size(axis)
    first, last = (max(0, -steps), min(count, count - steps))
    return lax.ppermute(value, axis, [(source, source + steps) for source in range(first, last)])


def local(top_grad, activations, weights, proj_in, proj_out, queries, lengths):
    sections = lax.axis_size("section")
    section_id = lax.axis_index("section")
    seq_count = lengths.shape[0]
    tok_rows = top_grad.shape[0]
    seq_len = tok_rows // seq_count
    features = top_grad.shape[1]
    in_proj = proj_in[0]
    out_proj = proj_out[0]
    sketch_dim = in_proj.shape[0]
    whole_weight = lax.all_gather(weights[0], "dp", axis=0, tiled=True)
    positions = lax.broadcasted_iota(jnp.int32, (seq_count, seq_len), 1)
    live_mask = (positions < lengths[:, None]).astype(jnp.float32).reshape(tok_rows, 1)
    top_masked = (top_grad.astype(jnp.float32) * live_mask).astype(jnp.bfloat16)
    length_f = lengths.astype(jnp.float32)
    x_proj = lax.dot_general(
        activations[0], in_proj, (((1,), (1,)), ((), ())), preferred_element_type=jnp.float32
    )
    x_proj = x_proj.astype(jnp.bfloat16).reshape(seq_count, seq_len, sketch_dim)

    def advance(operand):
        cotangent, slot_id = operand
        g_proj = lax.dot_general(
            cotangent, out_proj, (((1,), (1,)), ((), ())), preferred_element_type=jnp.float32
        ).astype(jnp.bfloat16)
        x_block = lax.dynamic_index_in_dim(x_proj, slot_id, 0, keepdims=False)
        sketch = lax.dot_general(
            g_proj, x_block, (((0,), (0,)), ((), ())), preferred_element_type=jnp.float32
        )
        sketch = sketch / lax.dynamic_index_in_dim(length_f, slot_id, 0, keepdims=False)
        backward = lax.dot_general(
            cotangent, whole_weight, (((1,), (1,)), ((), ())), preferred_element_type=jnp.float32
        )
        following = (cotangent.astype(jnp.float32) + backward).astype(jnp.bfloat16)
        return (sketch.astype(jnp.bfloat16).reshape(1, sketch_dim * sketch_dim), following)

    def skipped(operand):
        return (
            jnp.zeros((1, sketch_dim * sketch_dim), jnp.bfloat16),
            jnp.zeros((seq_len, features), jnp.bfloat16),
        )

    inbox = jnp.zeros((seq_len, features), jnp.bfloat16)
    sketches = jnp.zeros((seq_count, sketch_dim * sketch_dim), jnp.bfloat16)
    ticks = sections + seq_count - 1
    for tick in range(ticks):
        micro_id = tick - (sections - 1 - section_id)
        active = jnp.logical_and(micro_id >= 0, micro_id < seq_count)
        slot_id = jnp.clip(micro_id, 0, seq_count - 1)
        fresh_grad = lax.dynamic_slice_in_dim(top_masked, slot_id * seq_len, seq_len, 0)
        cotangent = jnp.where(section_id == sections - 1, fresh_grad, inbox)
        sketch, following = lax.cond(active, advance, skipped, (cotangent, slot_id))
        updated = lax.dynamic_update_slice(sketches, sketch, (slot_id, jnp.int32(0)))
        sketches = jnp.where(active, updated, sketches)
        if tick < ticks - 1:
            inbox = passed_along(following, "section", -1)
    local_queries = queries[0]
    partial_value = lax.dot_general(
        sketches,
        lax.all_gather(local_queries, "dp", axis=0, tiled=True),
        (((1,), (1,)), ((), ())),
        preferred_element_type=jnp.float32,
    )
    return lax.psum_scatter(partial_value, "section", scatter_dimension=1, tiled=True) * 0.125


def solution(mesh):
    in_specs = (
        P("dp", None),
        P("section", "dp", None),
        P("section", "dp", None),
        P("section", None, None),
        P("section", None, None),
        P("section", "dp", None),
        P("dp"),
    )
    out_specs = P("dp", "section")
    return jax.shard_map(local, mesh=mesh, in_specs=in_specs, out_specs=out_specs, check_vma=False)
```

profile of v0, /device:TPU:1, one launch (start us, length us, event | category | flops | bytes accessed | tf_op | source)
XLA Modules:
  0.0 953.7 jit_solution(14985815408737297292)
XLA Ops:
  8.0 1.7 fusion.47
  9.8 3.3 multiply_convert_fusion
  13.1 557.6 %all-gather.5.cloned.1.call-done = bf16[1,3584,3584]{2,1,0:T(8,128)(2,1)} async-done(((bf16[1,56,3584]{2,1,0:T(8,128)(2,1)}), bf16[1,3584,3584]{2,1,0:T(8,128)(2,1)}) %all-gather.5.cloned.1.call-update) | async-done | bytes 25690128 | tf_op jit(solution)/shard_map/all_gather | solution.py:23
  570.9 0.9 copy-done.1
  571.8 3.0 collective-permute-start
  574.8 13.6 %collective-permute-done = bf16[128,3584]{1,0:T(8,128)(2,1)S(1)} collective-permute-done((bf16[128,3584]{1,0:T(8,128)(2,1)}, bf16[128,3584]{1,0:T(8,128)(2,1)S(1)}, u32[]{:S(2)}, u32[]{:S(2)}) %collective-permute-start) | collective-permute-done | bytes 917536 | tf_op jit(solution)/shard_map/ppermute | solution.py:10
  588.3 1.0 conditional.6
  588.4 1.0 broadcast.45
  589.3 1.9 collective-permute-start.1
  592.0 33.1 %collective-permute-done.1 = bf16[128,3584]{1,0:T(8,128)(2,1)S(1)} collective-permute-done((bf16[128,3584]{1,0:T(8,128)(2,1)}, bf16[128,3584]{1,0:T(8,128)(2,1)S(1)}, u32[]{:S(2)}, u32[]{:S(2)}) %collective-permute-start.1) | collective-permute-done | bytes 917536 | tf_op jit(solution)/shard_map/ppermute | solution.py:10
  625.1 17.4 %conditional.7 = (bf16[1,4096]{1,0:T(2,128)(2,1)S(1)}, bf16[128,3584]{1,0:T(8,128)(2,1)}) conditional(s32[]{:T(128)} %convert_element_type.135, () %tuple.72, (pred[]{:T(512)}, s32[]{:T(128)}, bf16[256,3584]{1,0:T(8,128)(2,1)}, bf16[128,3584]{1,0:T(8,128)(2,1)S(1)}, bf16[64,3584]{1,0:T(8,128)(2,1)S(1)}, /*index=5*/bf16[2,128,64]{1,0,2:T(2,128)(2,1)S(1)}, ...), branch_computations={%region_4.5_spmd, %region_5.6_spmd} | conditional | flops 3350872064 | bytes 32697460 | solution.py:64
  625.8 2.4 fusion.21
  628.3 14.2 %fusion.20 = bf16[128,3584]{1,0:T(8,128)(2,1)} fusion(bf16[3584,3584]{1,0:T(8,128)(2,1)} %get-tuple-element.429, bf16[128,3584]{1,0:T(8,128)(2,1)S(1)} %get-tuple-element.425, bf16[256,3584]{1,0:T(8,128)(2,1)} %get-tuple-element.423, s32[]{:T(128)S(6)} %select_n.150, pred[]{:T(512)} %get-tuple-element.422), kind=kOutput, calls=%fused_computation.25 | convolution fusion | flops 3290628096 | bytes 30279680 | tf_op jit(solution)/shard_map/cond/branch_1_fun/dot_general | solution.py:43
  642.5 1.9 collective-permute-start.2
  644.7 16.3 %collective-permute-done.2 = bf16[128,3584]{1,0:T(8,128)(2,1)S(1)} collective-permute-done((bf16[128,3584]{1,0:T(8,128)(2,1)}, bf16[128,3584]{1,0:T(8,128)(2,1)S(1)}, u32[]{:S(2)}, u32[]{:S(2)}) %collective-permute-start.2) | collective-permute-done | bytes 917536 | tf_op jit(solution)/shard_map/ppermute | solution.py:10
  661.1 17.4 %conditional.8 = (bf16[1,4096]{1,0:T(2,128)(2,1)S(1)}, bf16[128,3584]{1,0:T(8,128)(2,1)}) conditional(s32[]{:T(128)} %convert_element_type.136, () %tuple.74, (pred[]{:T(512)}, s32[]{:T(128)}, bf16[256,3584]{1,0:T(8,128)(2,1)}, bf16[128,3584]{1,0:T(8,128)(2,1)S(1)}, bf16[64,3584]{1,0:T(8,128)(2,1)S(1)}, /*index=5*/bf16[2,128,64]{1,0,2:T(2,128)(2,1)S(1)}, ...), branch_computations={%region_6.7_spmd, %region_7.8_spmd} | conditional | flops 3350872064 | bytes 32697460 | solution.py:64
  661.8 2.4 fusion.28
  664.3 14.2 %fusion.27 = bf16[128,3584]{1,0:T(8,128)(2,1)} fusion(bf16[3584,3584]{1,0:T(8,128)(2,1)} %get-tuple-element.437, bf16[128,3584]{1,0:T(8,128)(2,1)S(1)} %get-tuple-element.433, bf16[256,3584]{1,0:T(8,128)(2,1)} %get-tuple-element.431, s32[]{:T(128)S(6)} %select_n.154, pred[]{:T(512)} %get-tuple-element.430), kind=kOutput, calls=%fused_computation.35 | convolution fusion | flops 3290628096 | bytes 30279680 | tf_op jit(solution)/shard_map/cond/branch_1_fun/dot_general | solution.py:43
  678.5 1.9 collective-permute-start.3
  680.8 16.1 %collective-permute-done.3 = bf16[128,3584]{1,0:T(8,128)(2,1)} collective-permute-done((bf16[128,3584]{1,0:T(8,128)(2,1)}, bf16[128,3584]{1,0:T(8,128)(2,1)}, u32[]{:S(2)}, u32[]{:S(2)}) %collective-permute-start.3) | collective-permute-done | bytes 917536 | tf_op jit(solution)/shard_map/ppermute | solution.py:10
  697.1 172.3 %all-gather.7.cloned.1.call-done = bf16[1,128,4096]{2,0,1:T(2,128)(2,1)} async-done(((bf16[1,2,4096]{2,0,1:T(2,128)(2,1)}), bf16[1,128,4096]{2,0,1:T(2,128)(2,1)}) %all-gather.7.cloned.1.call-update) | async-done | bytes 1048592 | tf_op jit(solution)/shard_map/all_gather | solution.py:72
  869.4 3.4 convolution_bitcast_fusion
  872.9 72.9 %reduce-scatter.4.cloned.1.call-done = f32[32,2]{1,0:T(8,128)} async-done(((f32[128,2]{1,0:T(8,128)}), f32[32,2]{1,0:T(8,128)}) %reduce-scatter.4.cloned.1.call-update) | async-done | bytes 272
  945.8 0.8 copy.26
  (43 shorter events, 5.4 us)
Async XLA Ops:
  6.5 1.5 copy-start
  6.5 3.2 copy-start.4
  6.5 564.2 %all-gather.5.cloned.1.call-start = ((), (), s32[]{:S(2)}) async-start(), calls=%async_computation.1 | async-start | bytes 26091520 | tf_op jit(solution)/shard_map/all_gather | solution.py:23
  7.3 862.2 %all-gather.7.cloned.1.call-start = ((), (), s32[]{:S(2)}) async-start(), calls=%async_computation.2 | async-start | bytes 2129920 | tf_op jit(solution)/shard_map/all_gather | solution.py:72
  9.8 560.9 %copy-start.3 = (bf16[1,64,3584]{2,1,0:T(8,128)(2,1)S(1)}, bf16[1,64,3584]{2,1,0:T(8,128)(2,1)}, u32[]{:S(2)}) copy-start(bf16[1,64,3584]{2,1,0:T(8,128)(2,1)} %param.21) | copy-start | bytes 1376260
  570.8 0.9 copy-start.1
  571.8 16.6 %collective-permute-start = (bf16[128,3584]{1,0:T(8,128)(2,1)}, bf16[128,3584]{1,0:T(8,128)(2,1)S(1)}, u32[]{:S(2)}, u32[]{:S(2)}) collective-permute-start(bf16[128,3584]{1,0:T(8,128)(2,1)} %copy-done.1), channel_id=1, source_target_pairs={{64,0},{128,64},{192,128},{65,1},{129,65},{193,129},{66,2},{130,66... | collective-permute-start | bytes 2752520 | tf_op jit(solution)/shard_map/ppermute | solution.py:10
  588.3 2.9 copy-start.2
  589.3 35.7 %collective-permute-start.1 = (bf16[128,3584]{1,0:T(8,128)(2,1)}, bf16[128,3584]{1,0:T(8,128)(2,1)S(1)}, u32[]{:S(2)}, u32[]{:S(2)}) collective-permute-start(bf16[128,3584]{1,0:T(8,128)(2,1)} %get-tuple-element.456), channel_id=1, source_target_pairs={{64,0},{128,64},{192,128},{65,1},{129,65},{193,129},{66,2},{130,66... | collective-permute-start | bytes 2752520 | tf_op jit(solution)/shard_map/ppermute | solution.py:10
  591.9 353.9 %reduce-scatter.4.cloned.1.call-start = ((), (), s32[]{:S(2)}) async-start(), calls=%async_computation.3 | async-start | bytes 81920
  642.5 18.6 %collective-permute-start.2 = (bf16[128,3584]{1,0:T(8,128)(2,1)}, bf16[128,3584]{1,0:T(8,128)(2,1)S(1)}, u32[]{:S(2)}, u32[]{:S(2)}) collective-permute-start(bf16[128,3584]{1,0:T(8,128)(2,1)} %get-tuple-element.458), channel_id=1, source_target_pairs={{64,0},{128,64},{192,128},{65,1},{129,65},{193,129},{66,2},{130,66... | collective-permute-start | bytes 2752520 | tf_op jit(solution)/shard_map/ppermute | solution.py:10
  678.5 18.4 %collective-permute-start.3 = (bf16[128,3584]{1,0:T(8,128)(2,1)}, bf16[128,3584]{1,0:T(8,128)(2,1)}, u32[]{:S(2)}, u32[]{:S(2)}) collective-permute-start(bf16[128,3584]{1,0:T(8,128)(2,1)} %get-tuple-element.460), channel_id=1, source_target_pairs={{64,0},{128,64},{192,128},{65,1},{129,65},{193,129},{66,2},{130,66... | collective-permute-start | bytes 2752520 | tf_op jit(solution)/shard_map/ppermute | solution.py:10
Sparse Core Ops, SparseCore 0:
  9.1 561.5 all-gather.4
  592.0 277.3 all-gather.6
  873.0 72.7 reduce-scatter.3
where the time goes:
time: 954 us
  waiting for transfers between devices  883 us (93%)
  matrix products  38.3 us (4%)
  between operations  13.3 us (1%)
    all_gather x1, waiting for transfers between devices, local(): whole_weight = lax.all_gather(weights[0], 'dp', axis=0, tiled=True)  558 us
    all_gather x1, waiting for transfers between devices, local(): lax.all_gather(local_queries, 'dp', axis=0, tiled=True)  172 us
    ppermute x4, waiting for transfers between devices, passed_along(): lax.ppermute(value, axis, [(source, source + steps) for source in range(f...  79.1 us
    unnamed x4, waiting for transfers between devices  73.7 us
    dot_general x2, matrix products, advance(): lax.dot_general(cotangent, whole_weight, (((1,), (1,)), ((), ())), prefer...  28.4 us
  transfers between devices with their start and end apart: 7, of which 7 were waited for; matrix products, arithmetic and copies ran while one was open for 4% of the time, Pallas kernels for 0%

commit v1 on v0

v1 whole, which is shorter than its diff:
```python
import functools

import jax
import jax.numpy as jnp
from jax import lax
from jax.experimental import pallas as pl
from jax.experimental.pallas import tpu as pltpu
from jax.sharding import PartitionSpec as P

D = 3584
R = 64
ROWS = 56
SEQ = 128
TOK = 256
MESH = pl.DeviceIdType.MESH
F32 = jnp.float32
BF16 = jnp.bfloat16
OFFSETS = (4, 3, 5, 2, 6, 1, 7, 0)
PLANE = tuple((a, b) for a in (2, 1, 3, 0) for b in (1, 0) if a or b)


def nt(a, b):
    return lax.dot_general(a, b, (((1,), (1,)), ((), ())), preferred_element_type=F32)


def kernel(
    top_ref, act_ref, w_ref, pin_ref, pout_ref, qry_ref, len_ref, out_ref,
    w_v, win_v, qry_v, pin_v, pout_v, act_v, top_v,
    wt, le, rr, s0_s, s0_r, ob, pb, zs, zb, ag, qb, qf, qg, acc, x2, skf, flat, ex_s, ex_r,
    ld, s0_ss, s0_rs, p_ss, p_rs, z_ss, z_rs, az_ss, az_rs, ap_ss, ap_rs, qz_ss, qz_rs, qp_ss, qp_rs, ex_ss, ex_rs,
):
    s = lax.axis_index("section")
    d = lax.axis_index("dp")
    z = lax.div(d, 8)
    p = lax.rem(d, 8)
    y = lax.div(p, 2)
    x = lax.rem(p, 2)
    lane = lax.broadcasted_iota(jnp.int32, (32, 128), 1)
    low = lane < 64

    def plane(a, b):
        return 2 * lax.rem(y + a, 4) + lax.rem(x + b, 2)

    def remote(src, dst, ss, rs, section, at_z, at_p):
        return pltpu.make_async_remote_copy(
            src_ref=src, dst_ref=dst, send_sem=ss, recv_sem=rs,
            device_id=(section, at_z * 8 + at_p), device_id_type=MESH,
        )

    def wait_bytes(ref, sem):
        pltpu.make_async_copy(ref, ref, sem).wait()

    bar = pltpu.get_barrier_semaphore()
    for dz in OFFSETS:
        for ds in (2, 3, 1, 0):
            if dz or ds:
                pl.semaphore_signal(
                    bar, inc=1, device_id=(lax.rem(s + ds, 4), lax.rem(z + dz, 8) * 8 + p), device_id_type=MESH
                )
    for a, b in PLANE:
        pl.semaphore_signal(bar, inc=1, device_id=(s, z * 8 + plane(a, b)), device_id_type=MESH)

    tile = jnp.minimum(lax.div(ROWS * d, 128), D // 128 - 2)
    loads = [
        pltpu.make_async_copy(pout_ref.at[0, :, pl.ds(pl.multiple_of(tile * 128, 128), 256)], win_v, ld.at[0]),
        pltpu.make_async_copy(w_ref.at[0], w_v, ld.at[1]),
        pltpu.make_async_copy(qry_ref.at[0], qry_v, ld.at[2]),
        pltpu.make_async_copy(act_ref.at[0], act_v, ld.at[3]),
        pltpu.make_async_copy(pin_ref.at[0], pin_v.at[pl.ds(0, R)], ld.at[4]),
        pltpu.make_async_copy(pin_ref.at[0], pin_v.at[pl.ds(R, R)], ld.at[5]),
        pltpu.make_async_copy(top_ref, top_v, ld.at[6]),
        pltpu.make_async_copy(pout_ref.at[0], pout_v.at[pl.ds(0, R)], ld.at[7]),
        pltpu.make_async_copy(pout_ref.at[0], pout_v.at[pl.ds(R, R)], ld.at[8]),
    ]
    for c in loads:
        c.start()

    loads[0].wait()
    first = ROWS * d - 128 * tile
    row = lax.broadcasted_iota(jnp.int32, (32, 256), 0)
    col = lax.broadcasted_iota(jnp.int32, (32, 256), 1) - first
    pick_low = jnp.where(col == row, 1.0, 0.0).astype(BF16)
    pick_high = jnp.where((col == row + 32) & (row < ROWS - 32), 1.0, 0.0).astype(BF16)
    window = win_v[...]
    both = jnp.concatenate([window, window], axis=0)
    s0_s[...] = jnp.where(low, nt(pick_low, both), nt(pick_high, both)).astype(BF16)

    loads[1].wait()

    @pl.when(s >= 1)
    def _():
        @pl.loop(0, D // 128)
        def _(c):
            part = w_v[:, pl.ds(pl.multiple_of(c * 128, 128), 128)].astype(F32)
            gap = jnp.zeros((R - ROWS, 128), F32)
            wt[pl.ds(pl.multiple_of(c * 128, 128), 128), :] = jnp.concatenate([part, gap, part, gap], axis=0).T

        wt[pl.ds(D, 16), :] = jnp.zeros((16, 128), F32)

        @pl.when(s < 3)
        def _():
            @pl.loop(0, 64)
            def _(c):
                one = wt[pl.ds(pl.multiple_of(c * ROWS, 8), 32), :]
                two = wt[pl.ds(pl.multiple_of(c * ROWS + 32, 8), 32), :]
                le[pl.ds(pl.multiple_of(c * 32, 32), 32), pl.ds(0, 128)] = jnp.where(low, one, two).astype(BF16)

        @pl.when(s == 3)
        def _():
            @pl.loop(0, 56)
            def _(c):
                at = lax.div(c, 4) * 256 + lax.rem(c, 4) * 32
                one = wt[pl.ds(pl.multiple_of(at, 32), 32), :]
                two = wt[pl.ds(pl.multiple_of(at + 128, 32), 32), :]
                le[pl.ds(pl.multiple_of(c * 32, 32), 32), pl.ds(0, 128)] = jnp.where(low, one, two).astype(BF16)

            le[pl.ds(1792, 256), pl.ds(0, 128)] = jnp.zeros((256, 128), BF16)

        lane_i = jnp.bitwise_and(lane, 63)
        half = jnp.right_shift(lane, 6)
        sub = lax.broadcasted_iota(jnp.int32, (32, 128), 0)

        @pl.loop(0, 64)
        def _(c):
            inner = ROWS * c + sub + 32 * half
            last = lax.div(c, 4) * 256 + lax.rem(c, 4) * 32 + sub + 128 * half
            at = jnp.where(s == 3, last, inner) - ROWS * d
            hit = (at == lane_i) & (lane_i < ROWS)
            le[pl.ds(pl.multiple_of(c * 32, 32), 32), pl.ds(128, 128)] = jnp.where(hit, 1.0, 0.0).astype(BF16)

    loads[2].wait()
    q32 = qry_v[...].astype(F32)
    for t in range(32):
        qf[pl.ds(t, 1), :] = q32[0:1, 128 * t:128 * t + 128]
        qf[pl.ds(32 + t, 1), :] = q32[1:2, 128 * t:128 * t + 128]
    qb[d] = qf[pl.ds(0, 64), :].astype(BF16)

    pl.semaphore_wait(bar, 38)

    @pl.when(s < 3)
    def _():
        remote(s0_s, s0_r, s0_ss, s0_rs, s + 1, z, p).start()

    def place(packed):
        turned = pltpu.roll(packed, 64, 1)
        zero = jnp.zeros((32, 128), F32)
        parts = (
            jnp.where(low, packed, zero), jnp.where(low, turned, zero),
            jnp.where(low, zero, turned), jnp.where(low, zero, packed),
        )
        for i, part in enumerate(parts):
            rr[pl.ds(32 * i, 32), :] = part.astype(BF16)
            rr[pl.ds(128 + 32 * i, 32), :] = part.astype(BF16)

    def summed(slot):
        wait_bytes(zb.at[slot], z_rs.at[slot])
        total = zb[slot, 0].astype(F32)
        for i in range(1, 8):
            total = total + zb[slot, i].astype(F32)
        return total

    def nth(i):
        return jnp.where(lax.rem(i, 2) == 1, 4 - lax.div(i + 1, 2), 4 + lax.div(i, 2))

    def spread(k):
        @pl.loop(0, 8)
        def _(i):
            to_z = lax.rem(z + nth(i), 8)
            at = pl.ds(pl.multiple_of(to_z * 256, 256), 256)
            ob[k, to_z] = jnp.dot(le[at, :], rr[...], preferred_element_type=F32).astype(BF16).reshape(8, 32, 128)
            for j, (a, b) in enumerate(PLANE):
                to_p = plane(a, b)
                remote(ob.at[k, to_z, to_p], pb.at[k, to_z, j], p_ss.at[k], p_rs.at[k, to_z], s, z, to_p).start()

    def relay(k):
        to_s = jnp.where(s == 3, 2 - k, s + 1)
        slot = jnp.where(s == 3, 1, k)

        @pl.loop(0, 8)
        def _(i):
            to_z = lax.rem(z + nth(i), 8)
            wait_bytes(pb.at[k, to_z], p_rs.at[k, to_z])
            total = ob[k, to_z, p].astype(F32)
            for j in range(7):
                total = total + pb[k, to_z, j].astype(F32)
            zs[k, to_z] = total.astype(BF16)
            remote(zs.at[k, to_z], zb.at[slot, z], z_ss.at[k], z_rs.at[slot], to_s, to_z, p).start()

    def projected(tokens, both_proj):
        acc[...] = jnp.zeros((TOK, 128), F32)

        @pl.loop(0, 7)
        def _(c):
            at = pl.ds(pl.multiple_of(c * 512, 512), 512)
            acc[...] += nt(tokens[:, at], both_proj[:, at])

    @pl.when(s >= 1)
    def _():
        wait_bytes(s0_r, s0_rs)
        place(s0_r[...].astype(F32))
        spread(0)

    for dz in OFFSETS[:-1]:
        to_z = lax.rem(z + dz, 8)
        remote(qb.at[d], qb.at[d], qz_ss, qz_rs, s, to_z, p).start()

    for c in loads[3:6]:
        c.wait()
    projected(act_v, pin_v)
    x2[...] = acc[...].astype(BF16)

    @pl.when(s >= 1)
    def _():
        relay(0)

    wait_bytes(qb.at[pl.ds(0, 7)], qz_rs)
    for a, b in PLANE:
        to_p = plane(a, b)

        @pl.loop(0, 8)
        def _(i):
            block = qb.at[i * 8 + p]
            remote(block, block, qp_ss, qp_rs, s, z, to_p).start()

    @pl.when(s >= 2)
    def _():
        place(summed(0))
        spread(1)
        relay(1)

    @pl.when(s == 3)
    def _():
        place(summed(1))
        spread(2)
        relay(2)

    wait_bytes(qb.at[pl.ds(0, 56)], qp_rs)

    @pl.loop(0, 64)
    def _(c):
        qf[pl.ds(pl.multiple_of(c * 64, 64), 64), :] = qb[c].astype(F32)

    for t in range(32):
        qg[:, 128 * t:128 * t + 128] = qf[pl.ds(t, 128, stride=32), :].astype(BF16)

    for c in loads[6:9]:
        c.wait()

    @pl.when(s == 3)
    def _():
        projected(top_v, pout_v)

    @pl.when(s < 3)
    def _():
        ag[d] = summed(1).astype(BF16)
        for dz in OFFSETS[:-1]:
            remote(ag.at[d], ag.at[d], az_ss, az_rs.at[z], s, lax.rem(z + dz, 8), p).start()

        for dz in (0, 1, 7, 2, 6, 3, 5, 4):
            from_z = lax.rem(z + dz, 8)
            block = ag.at[from_z * 8 + p]
            if dz:
                wait_bytes(block, az_rs.at[from_z])
            for a, b in PLANE:
                remote(block, block, ap_ss, ap_rs.at[from_z], s, z, plane(a, b)).start()
        acc[...] = jnp.zeros((TOK, 128), F32)
        wide = lax.broadcasted_iota(jnp.int32, (128, 128), 1) < 64
        for dz in (0, 1, 7, 2, 6, 3, 5, 4):
            from_z = lax.rem(z + dz, 8)
            wait_bytes(ag.at[pl.ds(0, 7)], ap_rs.at[from_z])

            @pl.when(from_z < 7)
            def _():
                for c in range(2):
                    piece = ag[pl.ds(from_z * 8 + 4 * c, 4)].reshape(128, 128)
                    zero = jnp.zeros_like(piece)
                    rhs = jnp.concatenate([jnp.where(wide, piece, zero), jnp.where(wide, zero, piece)], axis=0)
                    at = pl.ds(pl.multiple_of(from_z * 512 + 256 * c, 256), 256)
                    acc[...] += jnp.dot(top_v[:, at], rhs, preferred_element_type=F32)
        acc[...] = acc[...] + pltpu.roll(acc[...], 64, 1)

    position = lax.broadcasted_iota(jnp.int32, (SEQ, 128), 0)
    flat[...] = jnp.zeros((16, R * R), F32)
    for n in range(2):
        length = len_ref[n]
        rows = pl.ds(n * SEQ, SEQ)
        g = jnp.where(position < length, acc[rows, :], 0.0).astype(BF16)
        skf[...] = lax.dot_general(g, x2[rows, :], (((0,), (0,)), ((), ())), preferred_element_type=F32)
        pairs = jnp.where(low, skf[pl.ds(0, 32, stride=2), :], skf[pl.ds(1, 32, stride=2), :])
        pairs = pairs / jnp.full((32, 128), length, jnp.int32).astype(F32)
        for t in range(32):
            flat[pl.ds(n, 1), 128 * t:128 * t + 128] = pairs[t:t + 1, :]
    part = nt(flat[...].astype(BF16), qg[...])[0:8]
    ex_s[...] = part
    for j in range(1, 4):
        remote(ex_s, ex_r.at[j - 1], ex_ss, ex_rs, lax.rem(s + j, 4), z, p).start()
    wait_bytes(ex_r, ex_rs)
    total = ((part + ex_r[0]) + (ex_r[1] + ex_r[2])) * 0.125
    mine = jnp.zeros((8, 32), F32)
    for i in range(4):
        mine = mine + jnp.where(s == i, total[:, 32 * i:32 * i + 32], 0.0)
    out_ref[...] = mine[0:2, :]

    wait_bytes(ex_r, ex_ss)
    wait_bytes(qb.at[pl.ds(0, 7)], qz_ss)
    wait_bytes(qb.at[pl.ds(0, 56)], qp_ss)

    @pl.when(s < 3)
    def _():
        wait_bytes(s0_s, s0_ss)
        wait_bytes(ag.at[pl.ds(0, 7)], az_ss)
        wait_bytes(ag.at[pl.ds(0, 56)], ap_ss)

    for k in range(3):
        @pl.when(s >= k + 1)
        def _():
            wait_bytes(pb.at[k], p_ss.at[k])
            wait_bytes(zs.at[k], z_ss.at[k])


def local(top_grad, activations, weights, proj_in, proj_out, queries, lengths):
    dma = pltpu.SemaphoreType.DMA
    anywhere = pl.BlockSpec(memory_space=pl.ANY)
    return pl.pallas_call(
        kernel,
        out_shape=jax.ShapeDtypeStruct((2, 32), F32),
        in_specs=[anywhere] * 6 + [pl.BlockSpec(memory_space=pltpu.SMEM)],
        out_specs=pl.BlockSpec(memory_space=pltpu.VMEM),
        scratch_shapes=[
            pltpu.VMEM((ROWS, D), BF16),
            pltpu.VMEM((R, 256), BF16),
            pltpu.VMEM((2, R * R), BF16),
            pltpu.VMEM((2 * R, D), BF16),
            pltpu.VMEM((2 * R, D), BF16),
            pltpu.VMEM((TOK, D), BF16),
            pltpu.VMEM((TOK, D), BF16),
            pltpu.VMEM((D + 16, 128), F32),
            pltpu.VMEM((2048, 256), BF16),
            pltpu.VMEM((256, 128), BF16),
            pltpu.VMEM((32, 128), BF16),
            pltpu.VMEM((32, 128), BF16),
            pltpu.VMEM((3, 8, 8, 32, 128), BF16),
            pltpu.VMEM((3, 8, 7, 32, 128), BF16),
            pltpu.VMEM((3, 8, 32, 128), BF16),
            pltpu.VMEM((2, 8, 32, 128), BF16),
            pltpu.VMEM((64, 32, 128), BF16),
            pltpu.VMEM((64, 64, 128), BF16),
            pltpu.VMEM((4096, 128), F32),
            pltpu.VMEM((128, R * R), BF16),
            pltpu.VMEM((TOK, 128), F32),
            pltpu.VMEM((TOK, 128), BF16),
            pltpu.VMEM((128, 128), F32),
            pltpu.VMEM((16, R * R), F32),
            pltpu.VMEM((8, 128), F32),
            pltpu.VMEM((3, 8, 128), F32),
            dma((9,)),
            dma, dma,
            dma((3,)), dma((3, 8)),
            dma((3,)), dma((2,)),
            dma, dma((8,)),
            dma, dma((8,)),
            dma, dma, dma, dma,
            dma, dma,
        ],
        compiler_params=pltpu.CompilerParams(
            collective_id=0, has_side_effects=True, vmem_limit_bytes=48 * 2**20
        ),
        name="chain",
    )(top_grad, activations, weights, proj_in, proj_out, queries, lengths)


def solution(mesh):
    in_specs = (
        P("dp", None),
        P("section", "dp", None),
        P("section", "dp", None),
        P("section", None, None),
        P("section", None, None),
        P("section", "dp", None),
        P("dp"),
    )
    return jax.shard_map(local, mesh=mesh, in_specs=in_specs, out_specs=P("dp", "section"), check_vma=False)
```

time: 954 us -> 76.1 us (0.08)
  waiting for transfers between devices: 883 us -> 0 us
  Pallas kernels: 0 us -> 67.1 us
  matrix products: 38.3 us -> 0 us
  between operations: 13.3 us -> 0.02 us
    all_gather x2 -> x0, waiting for transfers between devices: 730 us -> none  [the longest x1 558 us: local(): whole_weight = lax.all_gather(weights[0], 'dp', axis=0, tiled=True)]
    ppermute x4 -> x0, waiting for transfers between devices: 79.1 us -> none  [passed_along(): lax.ppermute(value, axis, [(source, source + steps) for source in range(f...]
    unnamed x4 -> x0, waiting for transfers between devices: 73.7 us -> none
    pallas_call x0 -> x1, Pallas kernels: none -> 67.1 us  [local(): pl.pallas_call(kernel, out_shape=jax.ShapeDtypeStruct((2, 32), F32), in_s...]
    dot_general x5 -> x0, matrix products: 34.9 us -> none  [the longest x2 28.4 us: advance(): lax.dot_general(cotangent, whole_weight, (((1,), (1,)), ((), ())), prefer...]
  transfers between devices with their start and end apart: 7 -> 0, of which waited for: 7 -> 0; matrix products, arithmetic and copies ran while one was open for 4% -> 0% of each run, Pallas kernels for 0% -> 0%
where the time goes in v1:
time: 76.1 us; the launch traced here: 75.1 us
  Pallas kernels  67.1 us (88%)
  local copies, waits for them, and re-layouts  7.97 us (10%)
    pallas_call x1, Pallas kernels, local(): pl.pallas_call(kernel, out_shape=jax.ShapeDtypeStruct((2, 32), F32), in_s...  67.1 us
    unnamed x15, local copies, waits for them, and re-layouts  7.97 us

profile of v1, /device:TPU:1, one launch (start us, length us, event | category | flops | bytes accessed | tf_op | source)
XLA Modules:
  0.0 75.1 jit_solution(1182324512129513376)
XLA Ops:
  0.0 0.0 copy-start
  0.0 1.5 %copy-done = bf16[256,3584]{1,0:T(8,128)(2,1)S(1)} copy-done((bf16[256,3584]{1,0:T(8,128)(2,1)S(1)}, bf16[256,3584]{1,0:T(8,128)(2,1)}, u32[]{:S(2)}) %copy-start) | copy-done | bytes 1835032
  1.5 0.0 copy-start.1
  1.5 1.5 %copy-done.1 = bf16[1,256,3584]{2,1,0:T(8,128)(2,1)S(1)} copy-done((bf16[1,256,3584]{2,1,0:T(8,128)(2,1)S(1)}, bf16[1,256,3584]{2,1,0:T(8,128)(2,1)}, u32[]{:S(2)}) %copy-start.1) | copy-done | bytes 1835032
  3.0 0.0 copy-start.2
  3.0 1.0 %copy-done.2 = bf16[1,64,3584]{2,1,0:T(8,128)(2,1)S(1)} copy-done((bf16[1,64,3584]{2,1,0:T(8,128)(2,1)S(1)}, bf16[1,64,3584]{2,1,0:T(8,128)(2,1)}, u32[]{:S(2)}) %copy-start.2) | copy-done | bytes 458776
  4.0 0.0 copy-start.3
  4.0 1.0 %copy-done.3 = bf16[1,64,3584]{2,1,0:T(8,128)(2,1)S(1)} copy-done((bf16[1,64,3584]{2,1,0:T(8,128)(2,1)S(1)}, bf16[1,64,3584]{2,1,0:T(8,128)(2,1)}, u32[]{:S(2)}) %copy-start.3) | copy-done | bytes 458776
  5.0 0.0 copy-start.4
  5.0 1.0 %copy-done.4 = bf16[1,56,3584]{2,1,0:T(8,128)(2,1)S(1)} copy-done((bf16[1,56,3584]{2,1,0:T(8,128)(2,1)S(1)}, bf16[1,56,3584]{2,1,0:T(8,128)(2,1)}, u32[]{:S(2)}) %copy-start.4) | copy-done | bytes 401432
  6.0 0.0 copy-start.5
  6.0 0.7 copy-done.5
  6.8 0.0 copy-start.6
  6.8 0.7 copy-done.6
  7.4 67.1 %chain.1 = f32[2,32]{1,0:T(2,128)S(1)} custom-call(bf16[256,3584]{1,0:T(8,128)(2,1)S(1)} %copy-done, bf16[1,256,3584]{2,1,0:T(8,128)(2,1)S(1)} %copy-done.1, bf16[1,56,3584]{2,1,0:T(8,128)(2,1)S(1)} %copy-done.4, bf16[1,64,3584]{2,1,0:T(8,128)(2,1)S(1)} %copy-done.2, bf16[1,64,3584]{2,1,0:T(8,128)(2,1)S(1)} %copy-done.3, bf16[1,2,4096]{2,1,0:T(2,128)(2,1)S(1)} %copy-done.5, ...), custom_call_target="tpu_custom_call" | custom-call | tf_op jit(solution)/shard_map/chain/pallas_call | solution.py:324
  74.5 0.6 copy.9
Async XLA Ops:
  0.0 1.5 %copy-start = (bf16[256,3584]{1,0:T(8,128)(2,1)S(1)}, bf16[256,3584]{1,0:T(8,128)(2,1)}, u32[]{:S(2)}) copy-start(bf16[256,3584]{1,0:T(8,128)(2,1)} %top_ref.1) | copy-start | bytes 5505028
  1.5 1.5 %copy-start.1 = (bf16[1,256,3584]{2,1,0:T(8,128)(2,1)S(1)}, bf16[1,256,3584]{2,1,0:T(8,128)(2,1)}, u32[]{:S(2)}) copy-start(bf16[1,256,3584]{2,1,0:T(8,128)(2,1)} %act_ref.1) | copy-start | bytes 5505028
  3.0 1.0 %copy-start.2 = (bf16[1,64,3584]{2,1,0:T(8,128)(2,1)S(1)}, bf16[1,64,3584]{2,1,0:T(8,128)(2,1)}, u32[]{:S(2)}) copy-start(bf16[1,64,3584]{2,1,0:T(8,128)(2,1)} %pin_ref.1) | copy-start | bytes 1376260
  4.0 1.0 %copy-start.3 = (bf16[1,64,3584]{2,1,0:T(8,128)(2,1)S(1)}, bf16[1,64,3584]{2,1,0:T(8,128)(2,1)}, u32[]{:S(2)}) copy-start(bf16[1,64,3584]{2,1,0:T(8,128)(2,1)} %pout_ref.1) | copy-start | bytes 1376260
  5.0 1.0 %copy-start.4 = (bf16[1,56,3584]{2,1,0:T(8,128)(2,1)S(1)}, bf16[1,56,3584]{2,1,0:T(8,128)(2,1)}, u32[]{:S(2)}) copy-start(bf16[1,56,3584]{2,1,0:T(8,128)(2,1)} %w_ref.1) | copy-start | bytes 1204228
  6.0 0.7 copy-start.5
  6.8 0.7 copy-start.6

commit v2 on v1

--- a/solution.py
+++ b/solution.py
@@ -27,7 +27,7 @@
     top_ref, act_ref, w_ref, pin_ref, pout_ref, qry_ref, len_ref, out_ref,
     w_v, win_v, qry_v, pin_v, pout_v, act_v, top_v,
     wt, le, rr, s0_s, s0_r, ob, pb, zs, zb, ag, qb, qf, qg, acc, x2, skf, flat, ex_s, ex_r,
-    ld, s0_ss, s0_rs, p_ss, p_rs, z_ss, z_rs, az_ss, az_rs, ap_ss, ap_rs, qz_ss, qz_rs, qp_ss, qp_rs, ex_ss, ex_rs,
+    ld, s0_ss, s0_rs, p_ss, p_rs, z_ss, z_rs, az_ss, az_rs, ap_ss, ap_rs, qz_ss, qz_rs, qp_ss, qp_rs, ex_ss, ex_rs, gate,
 ):
     s = lax.axis_index("section")
     d = lax.axis_index("dp")
@@ -51,12 +51,10 @@
         pltpu.make_async_copy(ref, ref, sem).wait()
 
     bar = pltpu.get_barrier_semaphore()
-    for dz in OFFSETS:
-        for ds in (2, 3, 1, 0):
-            if dz or ds:
-                pl.semaphore_signal(
-                    bar, inc=1, device_id=(lax.rem(s + ds, 4), lax.rem(z + dz, 8) * 8 + p), device_id_type=MESH
-                )
+    for dz in OFFSETS[:-1]:
+        pl.semaphore_signal(bar, inc=1, device_id=(s, lax.rem(z + dz, 8) * 8 + p), device_id_type=MESH)
+    for ds in (2, 3, 1):
+        pl.semaphore_signal(bar, inc=1, device_id=(lax.rem(s + ds, 4), d), device_id_type=MESH)
     for a, b in PLANE:
         pl.semaphore_signal(bar, inc=1, device_id=(s, z * 8 + plane(a, b)), device_id_type=MESH)
 
@@ -75,6 +73,20 @@
     for c in loads:
         c.start()
 
+    @pl.when(s >= 1)
+    def _():
+        lane_i = jnp.bitwise_and(lane, 63)
+        half = jnp.right_shift(lane, 6)
+        sub = lax.broadcasted_iota(jnp.int32, (32, 128), 0)
+
+        @pl.loop(0, 64)
+        def _(c):
+            inner = ROWS * c + sub + 32 * half
+            last = lax.div(c, 4) * 256 + lax.rem(c, 4) * 32 + sub + 128 * half
+            at = jnp.where(s == 3, last, inner) - ROWS * d
+            hit = (at == lane_i) & (lane_i < ROWS)
+            le[pl.ds(pl.multiple_of(c * 32, 32), 32), pl.ds(128, 128)] = jnp.where(hit, 1.0, 0.0).astype(BF16)
+
     loads[0].wait()
     first = ROWS * d - 128 * tile
     row = lax.broadcasted_iota(jnp.int32, (32, 256), 0)
@@ -116,18 +128,6 @@
 
             le[pl.ds(1792, 256), pl.ds(0, 128)] = jnp.zeros((256, 128), BF16)
 
-        lane_i = jnp.bitwise_and(lane, 63)
-        half = jnp.right_shift(lane, 6)
-        sub = lax.broadcasted_iota(jnp.int32, (32, 128), 0)
-
-        @pl.loop(0, 64)
-        def _(c):
-            inner = ROWS * c + sub + 32 * half
-            last = lax.div(c, 4) * 256 + lax.rem(c, 4) * 32 + sub + 128 * half
-            at = jnp.where(s == 3, last, inner) - ROWS * d
-            hit = (at == lane_i) & (lane_i < ROWS)
-            le[pl.ds(pl.multiple_of(c * 32, 32), 32), pl.ds(128, 128)] = jnp.where(hit, 1.0, 0.0).astype(BF16)
-
     loads[2].wait()
     q32 = qry_v[...].astype(F32)
     for t in range(32):
@@ -135,11 +135,14 @@
         qf[pl.ds(32 + t, 1), :] = q32[1:2, 128 * t:128 * t + 128]
     qb[d] = qf[pl.ds(0, 64), :].astype(BF16)
 
-    pl.semaphore_wait(bar, 38)
+    pl.semaphore_wait(bar, 17)
 
     @pl.when(s < 3)
     def _():
         remote(s0_s, s0_r, s0_ss, s0_rs, s + 1, z, p).start()
+
+    for dz in OFFSETS[:-1]:
+        remote(qb.at[d], qb.at[d], qz_ss, qz_rs, s, lax.rem(z + dz, 8), p).start()
 
     def place(packed):
         turned = pltpu.roll(packed, 64, 1)
@@ -194,54 +197,92 @@
             at = pl.ds(pl.multiple_of(c * 512, 512), 512)
             acc[...] += nt(tokens[:, at], both_proj[:, at])
 
+    def pass_queries(first):
+        for a, b in PLANE:
+            to_p = plane(a, b)
+
+            @pl.loop(first, first + 4)
+            def _(i):
+                block = qb.at[i * 8 + p]
+                remote(block, block, qp_ss, qp_rs, s, z, to_p).start()
+
+    def turn_queries():
+        wait_bytes(qb.at[pl.ds(0, 56)], qp_rs)
+
+        @pl.loop(0, 64)
+        def _(c):
+            qf[pl.ds(pl.multiple_of(c * 64, 64), 64), :] = qb[c].astype(F32)
+
+        for t in range(32):
+            qg[:, 128 * t:128 * t + 128] = qf[pl.ds(t, 128, stride=32), :].astype(BF16)
+
+    def go_ahead(to_s):
+        pl.semaphore_signal(gate, inc=1, device_id=(to_s, d), device_id_type=MESH)
+
     @pl.when(s >= 1)
     def _():
         wait_bytes(s0_r, s0_rs)
         place(s0_r[...].astype(F32))
         spread(0)
 
-    for dz in OFFSETS[:-1]:
-        to_z = lax.rem(z + dz, 8)
-        remote(qb.at[d], qb.at[d], qz_ss, qz_rs, s, to_z, p).start()
+    @pl.when(s == 1)
+    def _():
+        go_ahead(0)
+
+    wait_bytes(qb.at[pl.ds(0, 7)], qz_rs)
+
+    @pl.when(s >= 1)
+    def _():
+        relay(0)
+
+    @pl.when(s == 0)
+    def _():
+        pl.semaphore_wait(gate, 1)
+
+    @pl.when(s != 2)
+    def _():
+        pass_queries(0)
+
+    @pl.when(s < 2)
+    def _():
+        pass_queries(4)
 
     for c in loads[3:6]:
         c.wait()
     projected(act_v, pin_v)
     x2[...] = acc[...].astype(BF16)
 
-    @pl.when(s >= 1)
-    def _():
-        relay(0)
-
-    wait_bytes(qb.at[pl.ds(0, 7)], qz_rs)
-    for a, b in PLANE:
-        to_p = plane(a, b)
-
-        @pl.loop(0, 8)
-        def _(i):
-            block = qb.at[i * 8 + p]
-            remote(block, block, qp_ss, qp_rs, s, z, to_p).start()
-
     @pl.when(s >= 2)
     def _():
         place(summed(0))
+
+        @pl.when(s == 3)
+        def _():
+            pl.semaphore_wait(gate, 1)
+
         spread(1)
+
+        @pl.when(s == 2)
+        def _():
+            go_ahead(3)
+
         relay(1)
+
+    @pl.when(s == 2)
+    def _():
+        pass_queries(0)
+        pl.semaphore_wait(gate, 1)
 
     @pl.when(s == 3)
     def _():
         place(summed(1))
         spread(2)
+        go_ahead(2)
         relay(2)
 
-    wait_bytes(qb.at[pl.ds(0, 56)], qp_rs)
-
-    @pl.loop(0, 64)
-    def _(c):
-        qf[pl.ds(pl.multiple_of(c * 64, 64), 64), :] = qb[c].astype(F32)
-
-    for t in range(32):
-        qg[:, 128 * t:128 * t + 128] = qf[pl.ds(t, 128, stride=32), :].astype(BF16)
+    @pl.when(s >= 2)
+    def _():
+        pass_queries(4)
 
     for c in loads[6:9]:
         c.wait()
@@ -249,35 +290,49 @@
     @pl.when(s == 3)
     def _():
         projected(top_v, pout_v)
+
+    @pl.when(s < 2)
+    def _():
+        turn_queries()
 
     @pl.when(s < 3)
     def _():
         ag[d] = summed(1).astype(BF16)
         for dz in OFFSETS[:-1]:
             remote(ag.at[d], ag.at[d], az_ss, az_rs.at[z], s, lax.rem(z + dz, 8), p).start()
-
-        for dz in (0, 1, 7, 2, 6, 3, 5, 4):
+        acc[...] = jnp.zeros((TOK, 128), F32)
+        wide = lax.broadcasted_iota(jnp.int32, (128, 128), 1) < 64
+
+        def forward(dz):
             from_z = lax.rem(z + dz, 8)
             block = ag.at[from_z * 8 + p]
             if dz:
                 wait_bytes(block, az_rs.at[from_z])
             for a, b in PLANE:
                 remote(block, block, ap_ss, ap_rs.at[from_z], s, z, plane(a, b)).start()
-        acc[...] = jnp.zeros((TOK, 128), F32)
-        wide = lax.broadcasted_iota(jnp.int32, (128, 128), 1) < 64
-        for dz in (0, 1, 7, 2, 6, 3, 5, 4):
+
+        def add(dz):
             from_z = lax.rem(z + dz, 8)
             wait_bytes(ag.at[pl.ds(0, 7)], ap_rs.at[from_z])
 
             @pl.when(from_z < 7)
             def _():
+                parts = []
                 for c in range(2):
                     piece = ag[pl.ds(from_z * 8 + 4 * c, 4)].reshape(128, 128)
                     zero = jnp.zeros_like(piece)
-                    rhs = jnp.concatenate([jnp.where(wide, piece, zero), jnp.where(wide, zero, piece)], axis=0)
-                    at = pl.ds(pl.multiple_of(from_z * 512 + 256 * c, 256), 256)
-                    acc[...] += jnp.dot(top_v[:, at], rhs, preferred_element_type=F32)
+                    parts += [jnp.where(wide, piece, zero), jnp.where(wide, zero, piece)]
+                at = pl.ds(pl.multiple_of(from_z * 512, 512), 512)
+                acc[...] += jnp.dot(top_v[:, at], jnp.concatenate(parts, axis=0), preferred_element_type=F32)
+
+        for step, dz in ((forward, 0), (forward, 1), (forward, 7), (forward, 2), (forward, 6), (add, 0), (forward, 3), (forward, 5),
+                         (add, 1), (forward, 4), (add, 7), (add, 2), (add, 6), (add, 3), (add, 5), (add, 4)):
+            step(dz)
         acc[...] = acc[...] + pltpu.roll(acc[...], 64, 1)
+
+    @pl.when(s >= 2)
+    def _():
+        turn_queries()
 
     position = lax.broadcasted_iota(jnp.int32, (SEQ, 128), 0)
     flat[...] = jnp.zeros((16, R * R), F32)
@@ -361,9 +416,10 @@
             dma, dma((8,)),
             dma, dma, dma, dma,
             dma, dma,
+            pltpu.SemaphoreType.REGULAR,
         ],
         compiler_params=pltpu.CompilerParams(
-            collective_id=0, has_side_effects=True, vmem_limit_bytes=48 * 2**20
+            collective_id=0, has_side_effects=True, vmem_limit_bytes=64 * 2**20 - 2**17
         ),
         name="chain",
     )(top_grad, activations, weights, proj_in, proj_out, queries, lengths)

time: 76.1 us -> 60.9 us (0.80)
  Pallas kernels: 67.1 us -> 59.3 us
  local copies, waits for them, and re-layouts: 7.97 us -> 1.24 us
    pallas_call x1, Pallas kernels: 67.1 us -> 59.3 us  [local(): pl.pallas_call(kernel, out_shape=jax.ShapeDtypeStruct((2, 32), F32), in_s...]
    unnamed x15 -> x1, local copies, waits for them, and re-layouts: 7.97 us -> 1.24 us
where the time goes in v2:
time: 60.9 us; the launch traced here: 60.6 us
  Pallas kernels  59.3 us (97%)
  local copies, waits for them, and re-layouts  1.24 us (2%)
    pallas_call x1, Pallas kernels, local(): pl.pallas_call(kernel, out_shape=jax.ShapeDtypeStruct((2, 32), F32), in_s...  59.3 us
    unnamed x1, local copies, waits for them, and re-layouts  1.24 us

profile of v2, /device:TPU:1, one launch (start us, length us, event | category | flops | bytes accessed | tf_op | source)
XLA Modules:
  0.0 60.6 jit_solution(7126401467863532286)
XLA Ops:
  0.0 59.3 %chain.1 = f32[2,32]{1,0:T(2,128)} custom-call(bf16[256,3584]{1,0:T(8,128)(2,1)} %top_ref.1, bf16[1,256,3584]{2,1,0:T(8,128)(2,1)} %act_ref.1, bf16[1,56,3584]{2,1,0:T(8,128)(2,1)} %w_ref.1, bf16[1,64,3584]{2,1,0:T(8,128)(2,1)} %pin_ref.1, bf16[1,64,3584]{2,1,0:T(8,128)(2,1)} %pout_ref.1, bf16[1,2,4096]{2,1,0:T(2,128)(2,1)} %qry_ref.1, s32[2]{0:T(128)} %len_ref.1), custom_call_target="tpu_custom_call" | custom-call | tf_op jit(solution)/shard_map/chain/pallas_call | solution.py:379
  59.3 1.2 %copy.9 = f32[2,32]{1,0:T(2,128)} copy(f32[2,32]{1,0:T(2,128)} %chain.1) | data formatting | bytes 512

commit v3 on v2

v3 whole, which is shorter than its diff:
```python
import functools

import jax
import jax.numpy as jnp
from jax import lax
from jax.experimental import pallas as pl
from jax.experimental.pallas import tpu as pltpu
from jax.sharding import PartitionSpec as P

D = 3584
R = 64
ROWS = 56
SEQ = 128
TOK = 256
MESH = pl.DeviceIdType.MESH
F32 = jnp.float32
BF16 = jnp.bfloat16
OFFSETS = (4, 3, 5, 2, 6, 1, 7, 0)
PARTS = ((0, 1), (1, 3), (3, 5), (5, 8))
PLANE = tuple((a, b) for a in (2, 1, 3, 0) for b in (1, 0) if a or b)


def nt(a, b):
    return lax.dot_general(a, b, (((1,), (1,)), ((), ())), preferred_element_type=F32)


def kernel(
    top_ref, act_ref, w_ref, pin_ref, pout_ref, qry_ref, len_ref, out_ref,
    w_v, win_v, qry_v, pin_v, pout_v, act_v, top_v,
    wt, le, rr, s0_s, s0_r, ob, pb, zs, zb, ag, qb, q3, qf, qg, qg3, acc, x2, skf, sk_s, sk_r, flat, ex,
    ld, s0_ss, s0_rs, p_ss, p_rs, z_ss, z_rs, az_ss, az_rs, ap_ss, ap_rs, qz_ss, qz_rs, qp_ss, qp_rs,
    q3z_ss, q3z_rs, q3p_ss, q3p_rs, sk_ss, sk_rs, ex_ss, ex_rs, gate, line,
):
    s = lax.axis_index("section")
    d = lax.axis_index("dp")
    z = lax.div(d, 8)
    p = lax.rem(d, 8)
    y = lax.div(p, 2)
    x = lax.rem(p, 2)
    lane = lax.broadcasted_iota(jnp.int32, (32, 128), 1)
    low = lane < 64

    def plane(a, b):
        return 2 * lax.rem(y + a, 4) + lax.rem(x + b, 2)

    def remote(src, dst, ss, rs, section, at_z, at_p):
        return pltpu.make_async_remote_copy(
            src_ref=src, dst_ref=dst, send_sem=ss, recv_sem=rs,
            device_id=(section, at_z * 8 + at_p), device_id_type=MESH,
        )

    def wait_bytes(ref, sem):
        pltpu.make_async_copy(ref, ref, sem).wait()

    bar = pltpu.get_barrier_semaphore()
    for dz in OFFSETS[:-1]:
        pl.semaphore_signal(bar, inc=1, device_id=(s, lax.rem(z + dz, 8) * 8 + p), device_id_type=MESH)
    for ds in (2, 3, 1):
        pl.semaphore_signal(bar, inc=1, device_id=(lax.rem(s + ds, 4), d), device_id_type=MESH)
    for a, b in PLANE:
        pl.semaphore_signal(bar, inc=1, device_id=(s, z * 8 + plane(a, b)), device_id_type=MESH)

    tile = jnp.minimum(lax.div(ROWS * d, 128), D // 128 - 2)
    loads = [
        pltpu.make_async_copy(pout_ref.at[0, :, pl.ds(pl.multiple_of(tile * 128, 128), 256)], win_v, ld.at[0]),
        pltpu.make_async_copy(w_ref.at[0], w_v, ld.at[1]),
        pltpu.make_async_copy(qry_ref.at[0], qry_v, ld.at[2]),
        pltpu.make_async_copy(act_ref.at[0], act_v, ld.at[3]),
        pltpu.make_async_copy(pin_ref.at[0], pin_v.at[pl.ds(0, R)], ld.at[4]),
        pltpu.make_async_copy(pin_ref.at[0], pin_v.at[pl.ds(R, R)], ld.at[5]),
        pltpu.make_async_copy(top_ref, top_v, ld.at[6]),
        pltpu.make_async_copy(pout_ref.at[0], pout_v.at[pl.ds(0, R)], ld.at[7]),
        pltpu.make_async_copy(pout_ref.at[0], pout_v.at[pl.ds(R, R)], ld.at[8]),
    ]
    for c in loads:
        c.start()

    ag[pl.ds(56, 8)] = jnp.zeros((8, 32, 128), BF16)

    @pl.when(s >= 1)
    def _():
        lane_i = jnp.bitwise_and(lane, 63)
        half = jnp.right_shift(lane, 6)
        sub = lax.broadcasted_iota(jnp.int32, (32, 128), 0)
        le[:, pl.ds(128, 128)] = jnp.zeros((2048, 128), BF16)

        def ones(c, at):
            hit = (at - ROWS * d == lane_i) & (lane_i < ROWS)
            le[pl.ds(pl.multiple_of(c * 32, 32), 32), pl.ds(128, 128)] = jnp.where(hit, 1.0, 0.0).astype(BF16)

        @pl.when(s < 3)
        def _():
            ones(d, ROWS * d + sub + 32 * half)

        @pl.when(s == 3)
        def _():
            from_c = lax.div(ROWS * d, 256) * 4

            @pl.loop(0, 8)
            def _(i):
                c = from_c + i
                ones(c, lax.div(c, 4) * 256 + lax.rem(c, 4) * 32 + sub + 128 * half)

    loads[0].wait()
    first = ROWS * d - 128 * tile
    row = lax.broadcasted_iota(jnp.int32, (32, 256), 0)
    col = lax.broadcasted_iota(jnp.int32, (32, 256), 1) - first
    pick_low = jnp.where(col == row, 1.0, 0.0).astype(BF16)
    pick_high = jnp.where((col == row + 32) & (row < ROWS - 32), 1.0, 0.0).astype(BF16)
    window = win_v[...]
    both = jnp.concatenate([window, window], axis=0)
    s0_s[...] = jnp.where(low, nt(pick_low, both), nt(pick_high, both)).astype(BF16)

    loads[1].wait()

    @pl.when(s >= 1)
    def _():
        @pl.loop(0, D // 128, unroll=7)
        def _(c):
            part = w_v[:, pl.ds(pl.multiple_of(c * 128, 128), 128)].astype(F32)
            gap = jnp.zeros((R - ROWS, 128), F32)
            wt[pl.ds(pl.multiple_of(c * 128, 128), 128), :] = jnp.concatenate([part, gap, part, gap], axis=0).T

        wt[pl.ds(D, 16), :] = jnp.zeros((16, 128), F32)

        @pl.when(s < 3)
        def _():
            @pl.loop(0, 64, unroll=8)
            def _(c):
                one = wt[pl.ds(pl.multiple_of(c * ROWS, 8), 32), :]
                two = wt[pl.ds(pl.multiple_of(c * ROWS + 32, 8), 32), :]
                le[pl.ds(pl.multiple_of(c * 32, 32), 32), pl.ds(0, 128)] = jnp.where(low, one, two).astype(BF16)

        @pl.when(s == 3)
        def _():
            @pl.loop(0, 56, unroll=8)
            def _(c):
                at = lax.div(c, 4) * 256 + lax.rem(c, 4) * 32
                one = wt[pl.ds(pl.multiple_of(at, 32), 32), :]
                two = wt[pl.ds(pl.multiple_of(at + 128, 32), 32), :]
                le[pl.ds(pl.multiple_of(c * 32, 32), 32), pl.ds(0, 128)] = jnp.where(low, one, two).astype(BF16)

            le[pl.ds(1792, 256), pl.ds(0, 128)] = jnp.zeros((256, 128), BF16)

    pl.semaphore_wait(bar, 17)

    @pl.when(s < 3)
    def _():
        remote(s0_s, s0_r, s0_ss, s0_rs, s + 1, z, p).start()

    for dz in OFFSETS[:-1]:
        pl.semaphore_signal(line, inc=1, device_id=(s, lax.rem(z + dz, 8) * 8 + p), device_id_type=MESH)

    def place(packed):
        turned = pltpu.roll(packed, 64, 1)
        zero = jnp.zeros((32, 128), F32)
        parts = (
            jnp.where(low, packed, zero), jnp.where(low, turned, zero),
            jnp.where(low, zero, turned), jnp.where(low, zero, packed),
        )
        for i, part in enumerate(parts):
            rr[pl.ds(32 * i, 32), :] = part.astype(BF16)
            rr[pl.ds(128 + 32 * i, 32), :] = part.astype(BF16)

    def summed(slot):
        wait_bytes(zb.at[slot], z_rs.at[slot])
        total = zb[slot, 0].astype(F32)
        for i in range(1, 8):
            total = total + zb[slot, i].astype(F32)
        return total

    def spread(k):
        for part, (lo, hi) in enumerate(PARTS):
            for i in range(lo, hi):
                at = pl.ds(pl.multiple_of(lax.rem(z + OFFSETS[i], 8) * 256, 256), 256)
                ob[k, :, i] = jnp.dot(le[at, :], rr[...], preferred_element_type=F32).astype(BF16).reshape(8, 32, 128)
            for j, (a, b) in enumerate(PLANE):
                to_p = plane(a, b)
                span = pl.ds(lo, hi - lo)
                remote(ob.at[k, to_p, span], pb.at[k, j, span], p_ss.at[k], p_rs.at[k, part], s, z, to_p).start()

    def relay(k, midway=None, early=None):
        to_s = jnp.where(s == 3, 2 - k, s + 1)
        slot = jnp.where(s == 3, 1, k)
        for part, (lo, hi) in enumerate(PARTS):
            wait_bytes(pb.at[k, pl.ds(0, hi - lo), pl.ds(0, 7)], p_rs.at[k, part])
            if part == 0 and early is not None:
                early()
            for i in range(lo, hi):
                total = ob[k, p, i].astype(F32)
                for j in range(7):
                    total = total + pb[k, j, i].astype(F32)
                zs[k, i] = total.astype(BF16)
                to_z = lax.rem(z + OFFSETS[i], 8)
                remote(zs.at[k, i], zb.at[slot, z], z_ss.at[k], z_rs.at[slot], to_s, to_z, p).start()
            if part == 2 and midway is not None:
                midway()

    def projected(tokens, both_proj):
        acc[...] = jnp.zeros((TOK, 128), F32)

        @pl.loop(0, 7)
        def _(c):
            at = pl.ds(pl.multiple_of(c * 512, 512), 512)
            acc[...] += nt(tokens[:, at], both_proj[:, at])

    def pass_queries(held, ss, rs):
        for a, b in PLANE:
            to_p = plane(a, b)

            @pl.loop(0, 8)
            def _(i):
                block = held.at[i * 8 + p]
                remote(block, block, ss, rs, s, z, to_p).start()

    def turn_queries(held, rs, turned, blocks=56):
        wait_bytes(held.at[pl.ds(0, blocks)], rs)

        @pl.loop(0, 64)
        def _(c):
            qf[pl.ds(pl.multiple_of(c * 64, 64), 64), :] = held[c].astype(F32)

        for t in range(32):
            turned[:, 128 * t:128 * t + 128] = qf[pl.ds(t, 128, stride=32), :].astype(BF16)

    def go_ahead(to_s):
        pl.semaphore_signal(gate, inc=1, device_id=(to_s, d), device_id_type=MESH)

    def project_inputs():
        for c in loads[3:6]:
            c.wait()
        projected(act_v, pin_v)
        x2[...] = acc[...].astype(BF16)

    position = lax.broadcasted_iota(jnp.int32, (SEQ, 128), 0)

    def sketch(n):
        length = len_ref[n]
        rows = pl.ds(n * SEQ, SEQ)
        g = jnp.where(position < length, acc[rows, :], 0.0).astype(BF16)
        skf[...] = lax.dot_general(g, x2[rows, :], (((0,), (0,)), ((), ())), preferred_element_type=F32)
        pairs = jnp.where(low, skf[pl.ds(0, 32, stride=2), :], skf[pl.ds(1, 32, stride=2), :])
        return pairs / jnp.full((32, 128), length, jnp.int32).astype(F32)

    def lay_flat(n, pairs, to):
        for t in range(32):
            to[pl.ds(n, 1), 128 * t:128 * t + 128] = pairs[t:t + 1, :]

    nearest = (0, 1, 7, 2, 6, 3, 5, 4)

    def gather_line():
        total = summed(1).astype(BF16)

        @pl.when(z < 7)
        def _():
            ag[d] = total
            for dz in OFFSETS[:-1]:
                remote(ag.at[d], ag.at[d], az_ss, az_rs.at[z], s, lax.rem(z + dz, 8), p).start()

    def gather_plane():
        for dz in nearest:
            from_z = lax.rem(z + dz, 8)

            @pl.when(from_z < 7)
            def _():
                block = ag.at[from_z * 8 + p]
                if dz:
                    wait_bytes(block, az_rs.at[from_z])
                for a, b in PLANE:
                    remote(block, block, ap_ss, ap_rs.at[from_z], s, z, plane(a, b)).start()

    def project_tokens():
        wide = lax.broadcasted_iota(jnp.int32, (128, 128), 1) < 64
        acc[...] = jnp.zeros((TOK, 128), F32)
        for group in ((0, 1, 7), (2, 6, 3, 5), (4,)):
            for dz in group:
                from_z = lax.rem(z + dz, 8)

                @pl.when(from_z < 7)
                def _():
                    wait_bytes(ag.at[pl.ds(0, 7)], ap_rs.at[from_z])

            total = acc[...]
            for dz in group:
                from_z = lax.rem(z + dz, 8)
                parts = []
                for c in range(2):
                    piece = ag[pl.ds(from_z * 8 + 4 * c, 4)].reshape(128, 128)
                    zero = jnp.zeros_like(piece)
                    parts += [jnp.where(wide, piece, zero), jnp.where(wide, zero, piece)]
                at = pl.ds(pl.multiple_of(lax.rem(from_z, 7) * 512, 512), 512)
                total = total + jnp.dot(top_v[:, at], jnp.concatenate(parts, axis=0), preferred_element_type=F32)
            acc[...] = total
        acc[...] = acc[...] + pltpu.roll(acc[...], 64, 1)

    @pl.when(s >= 1)
    def _():
        wait_bytes(s0_r, s0_rs)
        place(s0_r[...].astype(F32))

        spread(0)

        @pl.when(s == 1)
        def _():
            go_ahead(0)

    loads[2].wait()
    q32 = qry_v[...].astype(F32)
    for t in range(32):
        qf[pl.ds(t, 1), :] = q32[0:1, 128 * t:128 * t + 128]
        qf[pl.ds(32 + t, 1), :] = q32[1:2, 128 * t:128 * t + 128]
    qb[d] = qf[pl.ds(0, 64), :].astype(BF16)

    @pl.when(s < 2)
    def _():
        for dz in OFFSETS[:-1]:
            remote(qb.at[d], qb.at[d], qz_ss, qz_rs, s, lax.rem(z + dz, 8), p).start()

    def pass_across(first):
        @pl.loop(first, first + 4)
        def _(i):
            block = q3.at[i * 8 + p]
            for a, b in PLANE:
                remote(block, qb.at[i * 8 + p], q3p_ss, qp_rs, 2, z, plane(a, b)).start()

            @pl.when(i != z)
            def _():
                remote(block, qb.at[i * 8 + p], q3p_ss, qp_rs, 2, z, p).start()

    def pass_across_early():
        @pl.when(s == 3)
        def _():
            wait_bytes(q3.at[pl.ds(0, 8)], q3z_rs)
            pass_across(0)

    pl.semaphore_wait(line, 7)

    @pl.when(s == 2)
    def _():
        for dz in OFFSETS:
            remote(qb.at[d], q3.at[d], qz_ss, q3z_rs, 3, lax.rem(z + dz, 8), p).start()

    @pl.when(s == 3)
    def _():
        for dz in OFFSETS:
            remote(qb.at[d], q3.at[d], q3z_ss, q3z_rs, 1, lax.rem(z + dz, 8), p).start()

    @pl.when(s == 2)
    def _():
        place(summed(0))
        spread(1)

    @pl.when(s >= 1)
    def _():
        relay(0, early=pass_across_early)

    @pl.when(s == 2)
    def _():
        relay(1, lambda: go_ahead(3))
        project_inputs()
        gather_line()
        pl.semaphore_wait(gate, 1)

    @pl.when(s == 3)
    def _():
        place(summed(0))
        pl.semaphore_wait(gate, 1)
        spread(1)
        place(summed(1))
        spread(2)
        relay(1)
        relay(2, lambda: go_ahead(2))
        pass_across(4)
        project_inputs()
        for c in loads[6:9]:
            c.wait()
        projected(top_v, pout_v)
        for n in range(2):
            sk_s[pl.ds(32 * n, 32), :] = sketch(n).astype(BF16)
        remote(sk_s, sk_r, sk_ss, sk_rs, 1, z, p).start()

    @pl.when(s < 2)
    def _():
        @pl.when(s == 0)
        def _():
            pl.semaphore_wait(gate, 1)

        wait_bytes(qb.at[pl.ds(0, 7)], qz_rs)
        pass_queries(qb, qp_ss, qp_rs)

        @pl.when(s == 1)
        def _():
            wait_bytes(q3.at[pl.ds(0, 8)], q3z_rs)
            pass_queries(q3, q3p_ss, q3p_rs)

        project_inputs()
        turn_queries(qb, qp_rs, qg)

        @pl.when(s == 1)
        def _():
            turn_queries(q3, q3p_rs, qg3)

        gather_line()

    @pl.when(s < 3)
    def _():
        for c in loads[6:9]:
            c.wait()
        gather_plane()

        project_tokens()

        @pl.when(s == 2)
        def _():
            turn_queries(qb, qp_rs, qg, 63)

        flat[...] = jnp.zeros((16, R * R), F32)
        for n in range(2):
            lay_flat(n, sketch(n), flat)
        ex[s] = nt(flat[...].astype(BF16), qg[...])[0:8]

        @pl.when(s == 1)
        def _():
            wait_bytes(sk_r, sk_rs)
            for n in range(2):
                lay_flat(n, sk_r[pl.ds(32 * n, 32), :].astype(F32), flat)
            ex[s] += nt(flat[...].astype(BF16), qg3[...])[0:8]

        for j in (2, 3, 1):
            remote(ex.at[s], ex.at[s], ex_ss, ex_rs, lax.rem(s + j, 4), z, p).start()

    @pl.when(s < 3)
    def _():
        wait_bytes(ex.at[pl.ds(0, 2)], ex_rs)

    @pl.when(s == 3)
    def _():
        wait_bytes(ex, ex_rs)
    total = ex[0] + ex[1] + ex[2]
    mine = jnp.zeros((8, 32), F32)
    for i in range(4):
        mine = mine + jnp.where(s == i, total[:, 32 * i:32 * i + 32], 0.0)
    out_ref[...] = mine[0:2, :]

    @pl.when(s < 3)
    def _():
        wait_bytes(ex, ex_ss)
        wait_bytes(s0_s, s0_ss)
        wait_bytes(ag.at[pl.ds(0, 49)], ap_ss)

        @pl.when(z < 7)
        def _():
            wait_bytes(ag.at[pl.ds(0, 7)], az_ss)

    @pl.when(s < 2)
    def _():
        wait_bytes(qb.at[pl.ds(0, 7)], qz_ss)
        wait_bytes(qb.at[pl.ds(0, 56)], qp_ss)

    @pl.when(s == 2)
    def _():
        wait_bytes(qb.at[pl.ds(0, 8)], qz_ss)

    @pl.when(s == 1)
    def _():
        wait_bytes(q3.at[pl.ds(0, 56)], q3p_ss)

    @pl.when(s == 3)
    def _():
        wait_bytes(q3.at[pl.ds(0, 8)], q3z_ss)
        wait_bytes(qb.at[pl.ds(0, 63)], q3p_ss)
        wait_bytes(sk_s, sk_ss)

    for k in range(3):
        @pl.when(s > k)
        def _():
            wait_bytes(pb.at[k], p_ss.at[k])
            wait_bytes(zs.at[k], z_ss.at[k])


def local(top_grad, activations, weights, proj_in, proj_out, queries, lengths):
    dma = pltpu.SemaphoreType.DMA
    anywhere = pl.BlockSpec(memory_space=pl.ANY)
    return pl.pallas_call(
        kernel,
        out_shape=jax.ShapeDtypeStruct((2, 32), F32),
        in_specs=[anywhere] * 6 + [pl.BlockSpec(memory_space=pltpu.SMEM)],
        out_specs=pl.BlockSpec(memory_space=pltpu.VMEM),
        scratch_shapes=[
            pltpu.VMEM((ROWS, D), BF16),
            pltpu.VMEM((R, 256), BF16),
            pltpu.VMEM((2, R * R), BF16),
            pltpu.VMEM((2 * R, D), BF16),
            pltpu.VMEM((2 * R, D), BF16),
            pltpu.VMEM((TOK, D), BF16),
            pltpu.VMEM((TOK, D), BF16),
            pltpu.VMEM((D + 16, 128), F32),
            pltpu.VMEM((2048, 256), BF16),
            pltpu.VMEM((256, 128), BF16),
            pltpu.VMEM((32, 128), BF16),
            pltpu.VMEM((32, 128), BF16),
            pltpu.VMEM((3, 8, 8, 32, 128), BF16),
            pltpu.VMEM((3, 7, 8, 32, 128), BF16),
            pltpu.VMEM((3, 8, 32, 128), BF16),
            pltpu.VMEM((2, 8, 32, 128), BF16),
            pltpu.VMEM((64, 32, 128), BF16),
            pltpu.VMEM((64, 64, 128), BF16),
            pltpu.VMEM((64, 64, 128), BF16),
            pltpu.VMEM((4096, 128), F32),
            pltpu.VMEM((128, R * R), BF16),
            pltpu.VMEM((128, R * R), BF16),
            pltpu.VMEM((TOK, 128), F32),
            pltpu.VMEM((TOK, 128), BF16),
            pltpu.VMEM((128, 128), F32),
            pltpu.VMEM((64, 128), BF16),
            pltpu.VMEM((64, 128), BF16),
            pltpu.VMEM((16, R * R), F32),
            pltpu.VMEM((3, 8, 128), F32),
            dma((9,)),
            dma, dma,
            dma((3,)), dma((3, 4)),
            dma((3,)), dma((2,)),
            dma, dma((8,)),
            dma, dma((8,)),
            dma, dma, dma, dma,
            dma, dma, dma, dma, dma, dma,
            dma, dma,
            pltpu.SemaphoreType.REGULAR,
            pltpu.SemaphoreType.REGULAR,
        ],
        compiler_params=pltpu.CompilerParams(
            collective_id=0, has_side_effects=True, vmem_limit_bytes=64 * 2**20 - 2**17
        ),
        name="chain",
    )(top_grad, activations, weights, proj_in, proj_out, queries, lengths) * 0.125


def solution(mesh):
    in_specs = (
        P("dp", None),
        P("section", "dp", None),
        P("section", "dp", None),
        P("section", None, None),
        P("section", None, None),
        P("section", "dp", None),
        P("dp"),
    )
    return jax.shard_map(local, mesh=mesh, in_specs=in_specs, out_specs=P("dp", "section"), check_vma=False)
```

time: 60.9 us -> 55 us (0.903)
  the two profiles are of different devices: /device:TPU:1 before, /device:TPU:7 now
where the time goes in v3:
time: 55 us; the launch traced here: 54.9 us
  Pallas kernels  53.7 us (98%)
  other arithmetic  1.24 us (2%)
    pallas_call x1, Pallas kernels, local(): pl.pallas_call(kernel, out_shape=jax.ShapeDtypeStruct((2, 32), F32), in_s...  53.7 us
    mul x1, other arithmetic, local(): pl.pallas_call(kernel, out_shape=jax.ShapeDtypeStruct((2, 32), F32), in_s...  1.24 us

profile of v3, /device:TPU:7, one launch (start us, length us, event | category | flops | bytes accessed | tf_op | source)
XLA Modules:
  0.0 54.9 jit_solution(4356419637110027389)
XLA Ops:
  0.0 53.7 %chain.1 = f32[2,32]{1,0:T(2,128)} custom-call(bf16[256,3584]{1,0:T(8,128)(2,1)} %top_ref.1, bf16[1,256,3584]{2,1,0:T(8,128)(2,1)} %act_ref.1, bf16[1,56,3584]{2,1,0:T(8,128)(2,1)} %w_ref.1, bf16[1,64,3584]{2,1,0:T(8,128)(2,1)} %pin_ref.1, bf16[1,64,3584]{2,1,0:T(8,128)(2,1)} %pout_ref.1, bf16[1,2,4096]{2,1,0:T(2,128)(2,1)} %qry_ref.1, s32[2]{0:T(128)} %len_ref.1), custom_call_target="tpu_custom_call" | custom-call | tf_op jit(solution)/shard_map/chain/pallas_call | solution.py:484
  53.7 1.2 %broadcast_multiply_fusion = f32[2,32]{1,0:T(2,128)} fusion(f32[2,32]{1,0:T(2,128)} %chain.1), kind=kLoop, calls=%fused_computation | loop fusion | flops 64 | bytes 512 | tf_op jit(solution)/shard_map/mul | solution.py:484

commit v4 on v3

--- a/solution.py
+++ b/solution.py
@@ -27,9 +27,9 @@
 def kernel(
     top_ref, act_ref, w_ref, pin_ref, pout_ref, qry_ref, len_ref, out_ref,
     w_v, win_v, qry_v, pin_v, pout_v, act_v, top_v,
-    wt, le, rr, s0_s, s0_r, ob, pb, zs, zb, ag, qb, q3, qf, qg, qg3, acc, x2, skf, sk_s, sk_r, flat, ex,
+    wt, le, l3, lb, lc, rr, rb, r8, s0_s, s0_r, ob, pb, yz, yb, bs, ar_s, ar_r, zs, zb, ag, qb, q3, qf, qg, qg3, acc, x2, skf, sk_s, sk_r, flat, ex,
     ld, s0_ss, s0_rs, p_ss, p_rs, z_ss, z_rs, az_ss, az_rs, ap_ss, ap_rs, qz_ss, qz_rs, qp_ss, qp_rs,
-    q3z_ss, q3z_rs, q3p_ss, q3p_rs, sk_ss, sk_rs, ex_ss, ex_rs, gate, line,
+    wa_ss, wa_rs, v_ss, v_rs, y_ss, y_rs, ar_ss, ar_rs, q3z_ss, q3z_rs, q3p_ss, q3p_rs, sk_ss, sk_rs, ex_ss, ex_rs, gate, line,
 ):
     s = lax.axis_index("section")
     d = lax.axis_index("dp")
@@ -77,29 +77,15 @@
 
     ag[pl.ds(56, 8)] = jnp.zeros((8, 32, 128), BF16)
 
-    @pl.when(s >= 1)
-    def _():
-        lane_i = jnp.bitwise_and(lane, 63)
-        half = jnp.right_shift(lane, 6)
-        sub = lax.broadcasted_iota(jnp.int32, (32, 128), 0)
+    lane_i = jnp.bitwise_and(lane, 63)
+    half = jnp.right_shift(lane, 6)
+    sub = lax.broadcasted_iota(jnp.int32, (32, 128), 0)
+
+    @pl.when((s == 1) | (s == 2))
+    def _():
         le[:, pl.ds(128, 128)] = jnp.zeros((2048, 128), BF16)
-
-        def ones(c, at):
-            hit = (at - ROWS * d == lane_i) & (lane_i < ROWS)
-            le[pl.ds(pl.multiple_of(c * 32, 32), 32), pl.ds(128, 128)] = jnp.where(hit, 1.0, 0.0).astype(BF16)
-
-        @pl.when(s < 3)
-        def _():
-            ones(d, ROWS * d + sub + 32 * half)
-
-        @pl.when(s == 3)
-        def _():
-            from_c = lax.div(ROWS * d, 256) * 4
-
-            @pl.loop(0, 8)
-            def _(i):
-                c = from_c + i
-                ones(c, lax.div(c, 4) * 256 + lax.rem(c, 4) * 32 + sub + 128 * half)
+        hit = (sub + 32 * half == lane_i) & (lane_i < ROWS)
+        le[pl.ds(pl.multiple_of(d * 32, 32), 32), pl.ds(128, 128)] = jnp.where(hit, 1.0, 0.0).astype(BF16)
 
     loads[0].wait()
     first = ROWS * d - 128 * tile
@@ -133,14 +119,15 @@
 
         @pl.when(s == 3)
         def _():
-            @pl.loop(0, 56, unroll=8)
-            def _(c):
-                at = lax.div(c, 4) * 256 + lax.rem(c, 4) * 32
-                one = wt[pl.ds(pl.multiple_of(at, 32), 32), :]
-                two = wt[pl.ds(pl.multiple_of(at + 128, 32), 32), :]
-                le[pl.ds(pl.multiple_of(c * 32, 32), 32), pl.ds(0, 128)] = jnp.where(low, one, two).astype(BF16)
-
-            le[pl.ds(1792, 256), pl.ds(0, 128)] = jnp.zeros((256, 128), BF16)
+            @pl.loop(0, 7)
+            def _(i):
+                for j in range(8):
+                    at = 512 * i + 256 * (j // 4) + 32 * (j % 4)
+                    one = wt[pl.ds(pl.multiple_of(at, 32), 32), :]
+                    two = wt[pl.ds(pl.multiple_of(at + 128, 32), 32), :]
+                    l3[j, pl.ds(pl.multiple_of(i * 32, 32), 32), :] = jnp.where(low, one, two).astype(BF16)
+
+            l3[:, pl.ds(224, 32), :] = jnp.zeros((8, 32, 128), BF16)
 
     pl.semaphore_wait(bar, 17)
 
@@ -151,16 +138,20 @@
     for dz in OFFSETS[:-1]:
         pl.semaphore_signal(line, inc=1, device_id=(s, lax.rem(z + dz, 8) * 8 + p), device_id_type=MESH)
 
-    def place(packed):
+    def turned_parts(packed):
         turned = pltpu.roll(packed, 64, 1)
         zero = jnp.zeros((32, 128), F32)
-        parts = (
-            jnp.where(low, packed, zero), jnp.where(low, turned, zero),
-            jnp.where(low, zero, turned), jnp.where(low, zero, packed),
-        )
-        for i, part in enumerate(parts):
-            rr[pl.ds(32 * i, 32), :] = part.astype(BF16)
-            rr[pl.ds(128 + 32 * i, 32), :] = part.astype(BF16)
+        return [
+            part.astype(BF16) for part in (
+                jnp.where(low, packed, zero), jnp.where(low, turned, zero),
+                jnp.where(low, zero, turned), jnp.where(low, zero, packed),
+            )
+        ]
+
+    def place(packed):
+        for i, part in enumerate(turned_parts(packed)):
+            rr[pl.ds(32 * i, 32), :] = part
+            rr[pl.ds(128 + 32 * i, 32), :] = part
 
     def summed(slot):
         wait_bytes(zb.at[slot], z_rs.at[slot])
@@ -169,32 +160,68 @@
             total = total + zb[slot, i].astype(F32)
         return total
 
-    def spread(k):
+    def spread():
         for part, (lo, hi) in enumerate(PARTS):
             for i in range(lo, hi):
                 at = pl.ds(pl.multiple_of(lax.rem(z + OFFSETS[i], 8) * 256, 256), 256)
-                ob[k, :, i] = jnp.dot(le[at, :], rr[...], preferred_element_type=F32).astype(BF16).reshape(8, 32, 128)
+                ob[:, i] = jnp.dot(le[at, :], rr[...], preferred_element_type=F32).astype(BF16).reshape(8, 32, 128)
             for j, (a, b) in enumerate(PLANE):
                 to_p = plane(a, b)
                 span = pl.ds(lo, hi - lo)
-                remote(ob.at[k, to_p, span], pb.at[k, j, span], p_ss.at[k], p_rs.at[k, part], s, z, to_p).start()
-
-    def relay(k, midway=None, early=None):
-        to_s = jnp.where(s == 3, 2 - k, s + 1)
-        slot = jnp.where(s == 3, 1, k)
+                remote(ob.at[to_p, span], pb.at[j, span], p_ss, p_rs.at[part], s, z, to_p).start()
+
+    def relay():
         for part, (lo, hi) in enumerate(PARTS):
-            wait_bytes(pb.at[k, pl.ds(0, hi - lo), pl.ds(0, 7)], p_rs.at[k, part])
-            if part == 0 and early is not None:
-                early()
+            wait_bytes(pb.at[pl.ds(0, hi - lo), pl.ds(0, 7)], p_rs.at[part])
             for i in range(lo, hi):
-                total = ob[k, p, i].astype(F32)
+                total = ob[p, i].astype(F32)
                 for j in range(7):
-                    total = total + pb[k, j, i].astype(F32)
-                zs[k, i] = total.astype(BF16)
+                    total = total + pb[j, i].astype(F32)
+                zs[0, i] = total.astype(BF16)
                 to_z = lax.rem(z + OFFSETS[i], 8)
-                remote(zs.at[k, i], zb.at[slot, z], z_ss.at[k], z_rs.at[slot], to_s, to_z, p).start()
-            if part == 2 and midway is not None:
-                midway()
+                remote(zs.at[0, i], zb.at[0, z], z_ss.at[0], z_rs.at[0], s + 1, to_z, p).start()
+
+    def send_columns():
+        for dz in OFFSETS[:-1]:
+            to_z = lax.rem(z + dz, 8)
+            block = le.at[pl.ds(pl.multiple_of(to_z * 256, 256), 256), pl.ds(0, 128)]
+            remote(block, lb.at[z], wa_ss, wa_rs, s, to_z, p).start()
+        lb[z] = le[pl.ds(pl.multiple_of(z * 256, 256), 256), pl.ds(0, 128)]
+
+    def line_product():
+        for dz in nearest:
+            from_z = lax.rem(z + dz, 8)
+            if dz:
+                wait_bytes(yz.at[from_z], v_rs.at[from_z])
+            for i, part in enumerate(turned_parts(yz[from_z].astype(F32))):
+                rb[from_z, pl.ds(32 * i, 32), :] = part
+        wait_bytes(l3.at[pl.ds(0, 7)], wa_rs)
+        total = jnp.zeros((TOK, 128), F32)
+        for i in range(4):
+            left = jnp.concatenate([lb[2 * i], lb[2 * i + 1]], axis=1)
+            total = total + jnp.dot(left, rb[pl.ds(2 * i, 2)].reshape(256, 128), preferred_element_type=F32)
+        bs[...] = total.reshape(8, 32, 128)
+        bs[p] += yz[z].astype(F32)
+        ar_s[...] = bs[...].reshape(TOK, 128).astype(BF16)
+        for a, b in PLANE + ((0, 0),):
+            remote(ar_s, ar_r.at[p], ar_ss, ar_rs, 3, z, plane(a, b)).start()
+
+    def plane_product(k):
+        total = jnp.zeros((TOK, 128), F32)
+        for j in range(8):
+            for i, part in enumerate(turned_parts(yb[k, j].astype(F32))):
+                r8[j, pl.ds(32 * i, 32), :] = part
+                r8[j, pl.ds(128 + 32 * i, 32), :] = part
+        for j in range(8):
+            total = total + jnp.dot(lc[j], r8[j], preferred_element_type=F32)
+        zs[k] = total.astype(BF16).reshape(8, 32, 128)
+        for dz in OFFSETS:
+            to_z = lax.rem(z + dz, 8)
+            remote(zs.at[k, to_z], zb.at[1, z], z_ss.at[k], z_rs.at[1], 2 - k, to_z, p).start()
+
+    def share_plane(k):
+        for a, b in PLANE:
+            remote(yb.at[k, p], yb.at[k, p], y_ss.at[k], y_rs.at[k], s, z, plane(a, b)).start()
 
     def projected(tokens, both_proj):
         acc[...] = jnp.zeros((TOK, 128), F32)
@@ -293,16 +320,36 @@
             acc[...] = total
         acc[...] = acc[...] + pltpu.roll(acc[...], 64, 1)
 
-    @pl.when(s >= 1)
+    @pl.when(s == 2)
+    def _():
+        send_columns()
+
+    @pl.when((s == 1) | (s == 2))
     def _():
         wait_bytes(s0_r, s0_rs)
         place(s0_r[...].astype(F32))
-
-        spread(0)
+        spread()
 
         @pl.when(s == 1)
         def _():
             go_ahead(0)
+
+    @pl.when(s == 3)
+    def _():
+        for a, b in PLANE:
+            to_p = plane(a, b)
+            remote(l3.at[to_p], lc.at[p, :, pl.ds(0, 128)], wa_ss, wa_rs, s, z, to_p).start()
+        lc[p, :, 0:128] = l3[p]
+        wait_bytes(s0_r, s0_rs)
+        yb[0, p] = s0_r[...]
+        share_plane(0)
+
+        @pl.loop(0, 8)
+        def _(j):
+            for i in range(8):
+                at = 512 * i + lax.div(p, 4) * 256 + lax.rem(p, 4) * 32 + sub + 128 * half
+                hit = (at - ROWS * (8 * z + j) == lane_i) & (lane_i < ROWS)
+                lc[j, 32 * i:32 * i + 32, 128:256] = jnp.where(hit, 1.0, 0.0).astype(BF16)
 
     loads[2].wait()
     q32 = qry_v[...].astype(F32)
@@ -327,12 +374,6 @@
             def _():
                 remote(block, qb.at[i * 8 + p], q3p_ss, qp_rs, 2, z, p).start()
 
-    def pass_across_early():
-        @pl.when(s == 3)
-        def _():
-            wait_bytes(q3.at[pl.ds(0, 8)], q3z_rs)
-            pass_across(0)
-
     pl.semaphore_wait(line, 7)
 
     @pl.when(s == 2)
@@ -347,29 +388,39 @@
 
     @pl.when(s == 2)
     def _():
-        place(summed(0))
-        spread(1)
-
-    @pl.when(s >= 1)
-    def _():
-        relay(0, early=pass_across_early)
+        yz[z] = summed(0).astype(BF16)
+        for dz in OFFSETS[:-1]:
+            remote(yz.at[z], yz.at[z], v_ss, v_rs.at[z], s, lax.rem(z + dz, 8), p).start()
+
+    @pl.when((s == 1) | (s == 2))
+    def _():
+        relay()
 
     @pl.when(s == 2)
     def _():
-        relay(1, lambda: go_ahead(3))
+        line_product()
         project_inputs()
         gather_line()
         pl.semaphore_wait(gate, 1)
 
     @pl.when(s == 3)
     def _():
-        place(summed(0))
-        pl.semaphore_wait(gate, 1)
-        spread(1)
-        place(summed(1))
-        spread(2)
-        relay(1)
-        relay(2, lambda: go_ahead(2))
+        wait_bytes(l3.at[pl.ds(0, 7)], wa_rs)
+        wait_bytes(yb.at[0, pl.ds(0, 7)], y_rs.at[0])
+        plane_product(0)
+        wait_bytes(q3.at[pl.ds(0, 8)], q3z_rs)
+        pass_across(0)
+        yb[1, p] = summed(0).astype(BF16)
+        share_plane(1)
+        wait_bytes(yb.at[1, pl.ds(0, 7)], y_rs.at[1])
+        plane_product(1)
+        wait_bytes(ar_r, ar_rs)
+        total = ar_r[0].astype(F32)
+        for i in range(1, 8):
+            total = total + ar_r[i].astype(F32)
+        yb[2] = total.reshape(8, 32, 128).astype(BF16)
+        plane_product(2)
+        go_ahead(2)
         pass_across(4)
         project_inputs()
         for c in loads[6:9]:
@@ -396,10 +447,6 @@
         project_inputs()
         turn_queries(qb, qp_rs, qg)
 
-        @pl.when(s == 1)
-        def _():
-            turn_queries(q3, q3p_rs, qg3)
-
         gather_line()
 
     @pl.when(s < 3)
@@ -407,6 +454,10 @@
         for c in loads[6:9]:
             c.wait()
         gather_plane()
+
+        @pl.when(s == 1)
+        def _():
+            turn_queries(q3, q3p_rs, qg3)
 
         project_tokens()
 
@@ -471,11 +522,26 @@
         wait_bytes(qb.at[pl.ds(0, 63)], q3p_ss)
         wait_bytes(sk_s, sk_ss)
 
-    for k in range(3):
-        @pl.when(s > k)
-        def _():
-            wait_bytes(pb.at[k], p_ss.at[k])
+    @pl.when((s == 1) | (s == 2))
+    def _():
+        wait_bytes(pb, p_ss)
+        wait_bytes(zs.at[0], z_ss.at[0])
+
+    @pl.when(s >= 2)
+    def _():
+        wait_bytes(l3.at[pl.ds(0, 7)], wa_ss)
+
+    @pl.when(s == 2)
+    def _():
+        wait_bytes(yz.at[pl.ds(0, 7)], v_ss)
+        wait_bytes(ar_r, ar_ss)
+
+    @pl.when(s == 3)
+    def _():
+        for k in range(3):
             wait_bytes(zs.at[k], z_ss.at[k])
+        for k in range(2):
+            wait_bytes(yb.at[k, pl.ds(0, 7)], y_ss.at[k])
 
 
 def local(top_grad, activations, weights, proj_in, proj_out, queries, lengths):
@@ -496,11 +562,21 @@
             pltpu.VMEM((TOK, D), BF16),
             pltpu.VMEM((D + 16, 128), F32),
             pltpu.VMEM((2048, 256), BF16),
+            pltpu.VMEM((8, 256, 128), BF16),
+            pltpu.VMEM((8, 256, 128), BF16),
+            pltpu.VMEM((8, 256, 256), BF16),
             pltpu.VMEM((256, 128), BF16),
+            pltpu.VMEM((8, 128, 128), BF16),
+            pltpu.VMEM((8, 256, 128), BF16),
             pltpu.VMEM((32, 128), BF16),
             pltpu.VMEM((32, 128), BF16),
-            pltpu.VMEM((3, 8, 8, 32, 128), BF16),
-            pltpu.VMEM((3, 7, 8, 32, 128), BF16),
+            pltpu.VMEM((8, 8, 32, 128), BF16),
+            pltpu.VMEM((7, 8, 32, 128), BF16),
+            pltpu.VMEM((8, 32, 128), BF16),
+            pltpu.VMEM((3, 8, 32, 128), BF16),
+            pltpu.VMEM((8, 32, 128), F32),
+            pltpu.VMEM((TOK, 128), BF16),
+            pltpu.VMEM((8, TOK, 128), BF16),
             pltpu.VMEM((3, 8, 32, 128), BF16),
             pltpu.VMEM((2, 8, 32, 128), BF16),
             pltpu.VMEM((64, 32, 128), BF16),
@@ -518,11 +594,12 @@
             pltpu.VMEM((3, 8, 128), F32),
             dma((9,)),
             dma, dma,
-            dma((3,)), dma((3, 4)),
+            dma, dma((4,)),
             dma((3,)), dma((2,)),
             dma, dma((8,)),
             dma, dma((8,)),
             dma, dma, dma, dma,
+            dma, dma, dma, dma((8,)), dma((2,)), dma((2,)), dma, dma,
             dma, dma, dma, dma, dma, dma,
             dma, dma,
             pltpu.SemaphoreType.REGULAR,

time: 55 us -> 52.2 us (0.949)
  Pallas kernels: 53.7 us -> 50.9 us
    pallas_call x1, Pallas kernels: 53.7 us -> 50.9 us  [local(): pl.pallas_call(kernel, out_shape=jax.ShapeDtypeStruct((2, 32), F32), in_s...]
where the time goes in v4:
time: 52.2 us
  Pallas kernels  50.9 us (98%)
  other arithmetic  1.24 us (2%)
    pallas_call x1, Pallas kernels, local(): pl.pallas_call(kernel, out_shape=jax.ShapeDtypeStruct((2, 32), F32), in_s...  50.9 us
    mul x1, other arithmetic, local(): pl.pallas_call(kernel, out_shape=jax.ShapeDtypeStruct((2, 32), F32), in_s...  1.24 us

profile of v4, /device:TPU:7, one launch (start us, length us, event | category | flops | bytes accessed | tf_op | source)
XLA Modules:
  0.0 52.2 jit_solution(4279124536738942375)
XLA Ops:
  0.0 50.9 %chain.1 = f32[2,32]{1,0:T(2,128)} custom-call(bf16[256,3584]{1,0:T(8,128)(2,1)} %top_ref.1, bf16[1,256,3584]{2,1,0:T(8,128)(2,1)} %act_ref.1, bf16[1,56,3584]{2,1,0:T(8,128)(2,1)} %w_ref.1, bf16[1,64,3584]{2,1,0:T(8,128)(2,1)} %pin_ref.1, bf16[1,64,3584]{2,1,0:T(8,128)(2,1)} %pout_ref.1, bf16[1,2,4096]{2,1,0:T(2,128)(2,1)} %qry_ref.1, s32[2]{0:T(128)} %len_ref.1), custom_call_target="tpu_custom_call" | custom-call | tf_op jit(solution)/shard_map/chain/pallas_call | solution.py:550
  50.9 1.2 %broadcast_multiply_fusion = f32[2,32]{1,0:T(2,128)} fusion(f32[2,32]{1,0:T(2,128)} %chain.1), kind=kLoop, calls=%fused_computation | loop fusion | flops 64 | bytes 512 | tf_op jit(solution)/shard_map/mul | solution.py:550

commit v5 on v4

--- a/solution.py
+++ b/solution.py
@@ -27,9 +27,9 @@
 def kernel(
     top_ref, act_ref, w_ref, pin_ref, pout_ref, qry_ref, len_ref, out_ref,
     w_v, win_v, qry_v, pin_v, pout_v, act_v, top_v,
-    wt, le, l3, lb, lc, rr, rb, r8, s0_s, s0_r, ob, pb, yz, yb, bs, ar_s, ar_r, zs, zb, ag, qb, q3, qf, qg, qg3, acc, x2, skf, sk_s, sk_r, flat, ex,
+    wt, le, l3, lb, lc, rr, rb, r8, s0_s, s0_r, ob, pb, yz, yb, bs, ar_s, ar_r, zs, zb, ag, qown, qb, q3, qf, qg, qg3, acc, x2, xr, skf, sk_s, sk_r, flat, ex,
     ld, s0_ss, s0_rs, p_ss, p_rs, z_ss, z_rs, az_ss, az_rs, ap_ss, ap_rs, qz_ss, qz_rs, qp_ss, qp_rs,
-    wa_ss, wa_rs, v_ss, v_rs, y_ss, y_rs, ar_ss, ar_rs, q3z_ss, q3z_rs, q3p_ss, q3p_rs, sk_ss, sk_rs, ex_ss, ex_rs, gate, line,
+    wa_ss, wa_rs, v_ss, v_rs, y_ss, y_rs, ar_ss, ar_rs, q3z_rs, q3p_ss, q3p_rs, q3v_ss, q3v_rs, x_ss, x_rs, sk_ss, sk_rs, ex_ss, ex_rs, gate, line,
 ):
     s = lax.axis_index("section")
     d = lax.axis_index("dp")
@@ -153,8 +153,8 @@
             rr[pl.ds(32 * i, 32), :] = part
             rr[pl.ds(128 + 32 * i, 32), :] = part
 
-    def summed(slot):
-        wait_bytes(zb.at[slot], z_rs.at[slot])
+    def summed(slot, count=8):
+        wait_bytes(zb.at[slot, pl.ds(0, count)], z_rs.at[slot])
         total = zb[slot, 0].astype(F32)
         for i in range(1, 8):
             total = total + zb[slot, i].astype(F32)
@@ -217,7 +217,10 @@
         zs[k] = total.astype(BF16).reshape(8, 32, 128)
         for dz in OFFSETS:
             to_z = lax.rem(z + dz, 8)
-            remote(zs.at[k, to_z], zb.at[1, z], z_ss.at[k], z_rs.at[1], 2 - k, to_z, p).start()
+            if k == 2 and dz == 0:
+                zb[1, z] = zs[k, z]
+            else:
+                remote(zs.at[k, to_z], zb.at[1, z], z_ss.at[k], z_rs.at[1], (0, 1, 3)[k], to_z, p).start()
 
     def share_plane(k):
         for a, b in PLANE:
@@ -231,24 +234,29 @@
             at = pl.ds(pl.multiple_of(c * 512, 512), 512)
             acc[...] += nt(tokens[:, at], both_proj[:, at])
 
-    def pass_queries(held, ss, rs):
+    def pass_queries(held, ss, rs, first=0, count=8):
         for a, b in PLANE:
             to_p = plane(a, b)
 
-            @pl.loop(0, 8)
+            @pl.loop(first, first + count)
             def _(i):
                 block = held.at[i * 8 + p]
                 remote(block, block, ss, rs, s, z, to_p).start()
 
-    def turn_queries(held, rs, turned, blocks=56):
-        wait_bytes(held.at[pl.ds(0, blocks)], rs)
-
-        @pl.loop(0, 64)
+    def turn_queries(held, turned, first=0, count=8):
+        @pl.loop(8 * first, 8 * (first + count))
         def _(c):
             qf[pl.ds(pl.multiple_of(c * 64, 64), 64), :] = held[c].astype(F32)
 
         for t in range(32):
-            turned[:, 128 * t:128 * t + 128] = qf[pl.ds(t, 128, stride=32), :].astype(BF16)
+            rows = qf[pl.ds(512 * first + t, 16 * count, stride=32), :]
+            turned[128 * t:128 * t + 128, 16 * first:16 * (first + count)] = rows.T.astype(BF16)
+
+    def scored(turned):
+        return jnp.dot(flat[...].astype(BF16), turned[...], preferred_element_type=F32)[0:8]
+
+    def wait_queries(held, rs, blocks=56):
+        wait_bytes(held.at[pl.ds(0, blocks)], rs)
 
     def go_ahead(to_s):
         pl.semaphore_signal(gate, inc=1, device_id=(to_s, d), device_id_type=MESH)
@@ -261,11 +269,11 @@
 
     position = lax.broadcasted_iota(jnp.int32, (SEQ, 128), 0)
 
-    def sketch(n):
+    def sketch(n, held):
         length = len_ref[n]
         rows = pl.ds(n * SEQ, SEQ)
         g = jnp.where(position < length, acc[rows, :], 0.0).astype(BF16)
-        skf[...] = lax.dot_general(g, x2[rows, :], (((0,), (0,)), ((), ())), preferred_element_type=F32)
+        skf[...] = lax.dot_general(g, held[rows, :], (((0,), (0,)), ((), ())), preferred_element_type=F32)
         pairs = jnp.where(low, skf[pl.ds(0, 32, stride=2), :], skf[pl.ds(1, 32, stride=2), :])
         return pairs / jnp.full((32, 128), length, jnp.int32).astype(F32)
 
@@ -273,10 +281,11 @@
         for t in range(32):
             to[pl.ds(n, 1), 128 * t:128 * t + 128] = pairs[t:t + 1, :]
 
+    slot = jnp.minimum(s, 2)
     nearest = (0, 1, 7, 2, 6, 3, 5, 4)
 
-    def gather_line():
-        total = summed(1).astype(BF16)
+    def gather_line(count=8):
+        total = summed(1, count).astype(BF16)
 
         @pl.when(z < 7)
         def _():
@@ -299,7 +308,7 @@
     def project_tokens():
         wide = lax.broadcasted_iota(jnp.int32, (128, 128), 1) < 64
         acc[...] = jnp.zeros((TOK, 128), F32)
-        for group in ((0, 1, 7), (2, 6, 3, 5), (4,)):
+        for group in ((0, 1, 7), (2, 6), (3, 5), (4,)):
             for dz in group:
                 from_z = lax.rem(z + dz, 8)
 
@@ -356,135 +365,169 @@
     for t in range(32):
         qf[pl.ds(t, 1), :] = q32[0:1, 128 * t:128 * t + 128]
         qf[pl.ds(32 + t, 1), :] = q32[1:2, 128 * t:128 * t + 128]
-    qb[d] = qf[pl.ds(0, 64), :].astype(BF16)
-
-    @pl.when(s < 2)
+    qown[...] = qf[pl.ds(0, 64), :].astype(BF16)
+
+    @pl.when(s == 1)
+    def _():
+        qb[d] = qown[...]
+
+
+    @pl.when(s == 1)
     def _():
         for dz in OFFSETS[:-1]:
-            remote(qb.at[d], qb.at[d], qz_ss, qz_rs, s, lax.rem(z + dz, 8), p).start()
-
-    def pass_across(first):
-        @pl.loop(first, first + 4)
-        def _(i):
-            block = q3.at[i * 8 + p]
-            for a, b in PLANE:
-                remote(block, qb.at[i * 8 + p], q3p_ss, qp_rs, 2, z, plane(a, b)).start()
-
-            @pl.when(i != z)
-            def _():
-                remote(block, qb.at[i * 8 + p], q3p_ss, qp_rs, 2, z, p).start()
+            remote(qown, qb.at[d], qz_ss, qz_rs, s, lax.rem(z + dz, 8), p).start()
 
     pl.semaphore_wait(line, 7)
 
-    @pl.when(s == 2)
-    def _():
-        for dz in OFFSETS:
-            remote(qb.at[d], q3.at[d], qz_ss, q3z_rs, 3, lax.rem(z + dz, 8), p).start()
+    for at_s, to_s in ((0, 3), (2, 0)):
+        @pl.when(s == at_s)
+        def _():
+            for dz in OFFSETS:
+                remote(qown, qb.at[d], qz_ss, qz_rs, to_s, lax.rem(z + dz, 8), p).start()
 
     @pl.when(s == 3)
     def _():
-        for dz in OFFSETS:
-            remote(qb.at[d], q3.at[d], q3z_ss, q3z_rs, 1, lax.rem(z + dz, 8), p).start()
+        remote(qown, q3.at[d], qz_ss, q3z_rs, 1, z, p).start()
+
+    @pl.when((s == 1) | (s == 2))
+    def _():
+        relay()
 
     @pl.when(s == 2)
     def _():
         yz[z] = summed(0).astype(BF16)
         for dz in OFFSETS[:-1]:
             remote(yz.at[z], yz.at[z], v_ss, v_rs.at[z], s, lax.rem(z + dz, 8), p).start()
-
-    @pl.when((s == 1) | (s == 2))
-    def _():
-        relay()
-
-    @pl.when(s == 2)
-    def _():
         line_product()
         project_inputs()
-        gather_line()
-        pl.semaphore_wait(gate, 1)
+        remote(x2, xr, x_ss, x_rs, 0, z, p).start()
+        for c in loads[6:9]:
+            c.wait()
 
     @pl.when(s == 3)
     def _():
         wait_bytes(l3.at[pl.ds(0, 7)], wa_rs)
         wait_bytes(yb.at[0, pl.ds(0, 7)], y_rs.at[0])
         plane_product(0)
-        wait_bytes(q3.at[pl.ds(0, 8)], q3z_rs)
-        pass_across(0)
+        project_inputs()
+        for c in loads[6:9]:
+            c.wait()
+        projected(top_v, pout_v)
+        for n in range(2):
+            sk_s[pl.ds(32 * n, 32), :] = sketch(n, x2).astype(BF16)
+        remote(sk_s, sk_r, sk_ss, sk_rs, 1, z, p).start()
+        wait_bytes(qb.at[pl.ds(0, 8)], qz_rs)
+        pass_queries(qb, qp_ss.at[0], qp_rs.at[0], 0, 4)
         yb[1, p] = summed(0).astype(BF16)
         share_plane(1)
         wait_bytes(yb.at[1, pl.ds(0, 7)], y_rs.at[1])
         plane_product(1)
+        wait_queries(qb, qp_rs.at[0], 28)
+        turn_queries(qb, qg, 0, 4)
         wait_bytes(ar_r, ar_rs)
         total = ar_r[0].astype(F32)
         for i in range(1, 8):
             total = total + ar_r[i].astype(F32)
         yb[2] = total.reshape(8, 32, 128).astype(BF16)
         plane_product(2)
-        go_ahead(2)
-        pass_across(4)
+        pass_queries(qb, qp_ss.at[1], qp_rs.at[1], 4, 4)
+        gather_line(7)
+
+    def pass_own(blocks):
+        wait_bytes(qb.at[pl.ds(0, blocks)], qz_rs)
+        for i in range(2):
+            pass_queries(qb, qp_ss.at[i], qp_rs.at[i], 4 * i, 4)
+
+    @pl.when(s == 0)
+    def _():
+        pl.semaphore_wait(gate, 1)
+
+    @pl.when(s == 1)
+    def _():
+        wait_bytes(q3.at[0], q3z_rs)
+        for a, b in PLANE:
+            remote(q3.at[d], q3.at[d], q3p_ss, q3p_rs, s, z, plane(a, b)).start()
+        pass_own(7)
+
+    @pl.when(s < 2)
+    def _():
         project_inputs()
         for c in loads[6:9]:
             c.wait()
-        projected(top_v, pout_v)
-        for n in range(2):
-            sk_s[pl.ds(32 * n, 32), :] = sketch(n).astype(BF16)
-        remote(sk_s, sk_r, sk_ss, sk_rs, 1, z, p).start()
+
+    @pl.when(s == 1)
+    def _():
+        wait_bytes(q3.at[pl.ds(0, 7)], q3p_rs)
+        span = q3.at[pl.ds(pl.multiple_of(8 * z, 8), 8)]
+        for dz in OFFSETS[:-1]:
+            remote(span, span, q3v_ss, q3v_rs, s, lax.rem(z + dz, 8), p).start()
+
+    @pl.when(s == 0)
+    def _():
+        remote(x2, xr, x_ss, x_rs, 3, z, p).start()
+
+    def turn_own():
+        for i in range(2):
+            wait_queries(qb, qp_rs.at[i], 28)
+            turn_queries(qb, qg, 4 * i, 4)
+
+    @pl.when(s == 1)
+    def _():
+        turn_own()
 
     @pl.when(s < 2)
     def _():
-        @pl.when(s == 0)
-        def _():
-            pl.semaphore_wait(gate, 1)
-
-        wait_bytes(qb.at[pl.ds(0, 7)], qz_rs)
-        pass_queries(qb, qp_ss, qp_rs)
+        gather_line()
+
+    @pl.when(s == 0)
+    def _():
+        pass_own(8)
+
+    @pl.when(s != 2)
+    def _():
+        gather_plane()
+
+        @pl.when(s == 3)
+        def _():
+            wait_queries(qb, qp_rs.at[1], 28)
+            turn_queries(qb, qg, 4, 4)
 
         @pl.when(s == 1)
         def _():
-            wait_bytes(q3.at[pl.ds(0, 8)], q3z_rs)
-            pass_queries(q3, q3p_ss, q3p_rs)
-
-        project_inputs()
-        turn_queries(qb, qp_rs, qg)
-
-        gather_line()
-
-    @pl.when(s < 3)
-    def _():
-        for c in loads[6:9]:
-            c.wait()
-        gather_plane()
-
-        @pl.when(s == 1)
-        def _():
-            turn_queries(q3, q3p_rs, qg3)
+            wait_queries(q3, q3v_rs)
+            turn_queries(q3, qg3)
+            xr[...] = x2[...]
+
+        @pl.when(s != 1)
+        def _():
+            wait_bytes(xr, x_rs)
 
         project_tokens()
-
-        @pl.when(s == 2)
-        def _():
-            turn_queries(qb, qp_rs, qg, 63)
-
         flat[...] = jnp.zeros((16, R * R), F32)
         for n in range(2):
-            lay_flat(n, sketch(n), flat)
-        ex[s] = nt(flat[...].astype(BF16), qg[...])[0:8]
+            lay_flat(n, sketch(n, xr), flat)
+
+        @pl.when(s == 0)
+        def _():
+            turn_own()
+
+        ex[slot] = scored(qg)
 
         @pl.when(s == 1)
         def _():
             wait_bytes(sk_r, sk_rs)
             for n in range(2):
                 lay_flat(n, sk_r[pl.ds(32 * n, 32), :].astype(F32), flat)
-            ex[s] += nt(flat[...].astype(BF16), qg3[...])[0:8]
+            ex[slot] += scored(qg3)
 
         for j in (2, 3, 1):
-            remote(ex.at[s], ex.at[s], ex_ss, ex_rs, lax.rem(s + j, 4), z, p).start()
-
-    @pl.when(s < 3)
+            remote(ex.at[slot], ex.at[slot], ex_ss, ex_rs, lax.rem(s + j, 4), z, p).start()
+
+    @pl.when(s != 2)
     def _():
         wait_bytes(ex.at[pl.ds(0, 2)], ex_rs)
 
-    @pl.when(s == 3)
+    @pl.when(s == 2)
     def _():
         wait_bytes(ex, ex_rs)
     total = ex[0] + ex[1] + ex[2]
@@ -495,31 +538,39 @@
 
     @pl.when(s < 3)
     def _():
+        wait_bytes(s0_s, s0_ss)
+
+    @pl.when(s != 2)
+    def _():
         wait_bytes(ex, ex_ss)
-        wait_bytes(s0_s, s0_ss)
         wait_bytes(ag.at[pl.ds(0, 49)], ap_ss)
+        for i in range(2):
+            wait_bytes(qb.at[pl.ds(0, 28)], qp_ss.at[i])
 
         @pl.when(z < 7)
         def _():
             wait_bytes(ag.at[pl.ds(0, 7)], az_ss)
 
-    @pl.when(s < 2)
+    @pl.when(s == 1)
     def _():
         wait_bytes(qb.at[pl.ds(0, 7)], qz_ss)
-        wait_bytes(qb.at[pl.ds(0, 56)], qp_ss)
-
-    @pl.when(s == 2)
+        wait_bytes(q3.at[pl.ds(0, 7)], q3p_ss)
+        wait_bytes(q3.at[pl.ds(0, 56)], q3v_ss)
+
+    @pl.when(s == 3)
+    def _():
+        wait_bytes(qown, qz_ss)
+
+    @pl.when((s == 0) | (s == 2))
     def _():
         wait_bytes(qb.at[pl.ds(0, 8)], qz_ss)
 
-    @pl.when(s == 1)
-    def _():
-        wait_bytes(q3.at[pl.ds(0, 56)], q3p_ss)
+    @pl.when((s == 0) | (s == 2))
+    def _():
+        wait_bytes(xr, x_ss)
 
     @pl.when(s == 3)
     def _():
-        wait_bytes(q3.at[pl.ds(0, 8)], q3z_ss)
-        wait_bytes(qb.at[pl.ds(0, 63)], q3p_ss)
         wait_bytes(sk_s, sk_ss)
 
     @pl.when((s == 1) | (s == 2))
@@ -538,8 +589,9 @@
 
     @pl.when(s == 3)
     def _():
-        for k in range(3):
+        for k in range(2):
             wait_bytes(zs.at[k], z_ss.at[k])
+        wait_bytes(zs.at[2, pl.ds(0, 7)], z_ss.at[2])
         for k in range(2):
             wait_bytes(yb.at[k, pl.ds(0, 7)], y_ss.at[k])
 
@@ -580,12 +632,14 @@
             pltpu.VMEM((3, 8, 32, 128), BF16),
             pltpu.VMEM((2, 8, 32, 128), BF16),
             pltpu.VMEM((64, 32, 128), BF16),
+            pltpu.VMEM((64, 128), BF16),
             pltpu.VMEM((64, 64, 128), BF16),
             pltpu.VMEM((64, 64, 128), BF16),
             pltpu.VMEM((4096, 128), F32),
-            pltpu.VMEM((128, R * R), BF16),
-            pltpu.VMEM((128, R * R), BF16),
+            pltpu.VMEM((R * R, 128), BF16),
+            pltpu.VMEM((R * R, 128), BF16),
             pltpu.VMEM((TOK, 128), F32),
+            pltpu.VMEM((TOK, 128), BF16),
             pltpu.VMEM((TOK, 128), BF16),
             pltpu.VMEM((128, 128), F32),
             pltpu.VMEM((64, 128), BF16),
@@ -598,9 +652,9 @@
             dma((3,)), dma((2,)),
             dma, dma((8,)),
             dma, dma((8,)),
-            dma, dma, dma, dma,
+            dma, dma, dma((2,)), dma((2,)),
             dma, dma, dma, dma((8,)), dma((2,)), dma((2,)), dma, dma,
-            dma, dma, dma, dma, dma, dma,
+            dma, dma, dma, dma, dma, dma, dma, dma, dma,
             dma, dma,
             pltpu.SemaphoreType.REGULAR,
             pltpu.SemaphoreType.REGULAR,

time: 52.2 us -> 49.6 us (0.950)
  the two profiles are of different devices: /device:TPU:7 before, /device:TPU:1 now
where the time goes in v5:
time: 49.6 us; the launch traced here: 49.5 us
  Pallas kernels  48.2 us (97%)
  other arithmetic  1.24 us (2%)
    pallas_call x1, Pallas kernels, local(): pl.pallas_call(kernel, out_shape=jax.ShapeDtypeStruct((2, 32), F32), in_s...  48.2 us
    mul x1, other arithmetic, local(): pl.pallas_call(kernel, out_shape=jax.ShapeDtypeStruct((2, 32), F32), in_s...  1.24 us

profile of v5, /device:TPU:1, one launch (start us, length us, event | category | flops | bytes accessed | tf_op | source)
XLA Modules:
  0.0 49.5 jit_solution(17833531994214997225)
XLA Ops:
  0.0 48.2 %chain.1 = f32[2,32]{1,0:T(2,128)} custom-call(bf16[256,3584]{1,0:T(8,128)(2,1)} %top_ref.1, bf16[1,256,3584]{2,1,0:T(8,128)(2,1)} %act_ref.1, bf16[1,56,3584]{2,1,0:T(8,128)(2,1)} %w_ref.1, bf16[1,64,3584]{2,1,0:T(8,128)(2,1)} %pin_ref.1, bf16[1,64,3584]{2,1,0:T(8,128)(2,1)} %pout_ref.1, bf16[1,2,4096]{2,1,0:T(2,128)(2,1)} %qry_ref.1, s32[2]{0:T(128)} %len_ref.1), custom_call_target="tpu_custom_call" | custom-call | tf_op jit(solution)/shard_map/chain/pallas_call | solution.py:602
  48.3 1.2 %broadcast_multiply_fusion = f32[2,32]{1,0:T(2,128)} fusion(f32[2,32]{1,0:T(2,128)} %chain.1), kind=kLoop, calls=%fused_computation | loop fusion | flops 64 | bytes 512 | tf_op jit(solution)/shard_map/mul | solution.py:602

commit v6 on v5

--- a/solution.py
+++ b/solution.py
@@ -27,7 +27,7 @@
 def kernel(
     top_ref, act_ref, w_ref, pin_ref, pout_ref, qry_ref, len_ref, out_ref,
     w_v, win_v, qry_v, pin_v, pout_v, act_v, top_v,
-    wt, le, l3, lb, lc, rr, rb, r8, s0_s, s0_r, ob, pb, yz, yb, bs, ar_s, ar_r, zs, zb, ag, qown, qb, q3, qf, qg, qg3, acc, x2, xr, skf, sk_s, sk_r, flat, ex,
+    wt, le, l3, lb, lc, rr, s0_s, s0_r, ob, pb, yz, yb, bs, ar_s, ar_r, zs, zb, ag, qown, qb, q3, qf, qg, qg3, acc, x2, xr, skf, sk_s, sk_r, flat, ex,
     ld, s0_ss, s0_rs, p_ss, p_rs, z_ss, z_rs, az_ss, az_rs, ap_ss, ap_rs, qz_ss, qz_rs, qp_ss, qp_rs,
     wa_ss, wa_rs, v_ss, v_rs, y_ss, y_rs, ar_ss, ar_rs, q3z_rs, q3p_ss, q3p_rs, q3v_ss, q3v_rs, x_ss, x_rs, sk_ss, sk_rs, ex_ss, ex_rs, gate, line,
 ):
@@ -189,17 +189,14 @@
         lb[z] = le[pl.ds(pl.multiple_of(z * 256, 256), 256), pl.ds(0, 128)]
 
     def line_product():
+        wait_bytes(l3.at[pl.ds(0, 7)], wa_rs)
+        total = jnp.zeros((TOK, 128), F32)
         for dz in nearest:
             from_z = lax.rem(z + dz, 8)
             if dz:
                 wait_bytes(yz.at[from_z], v_rs.at[from_z])
-            for i, part in enumerate(turned_parts(yz[from_z].astype(F32))):
-                rb[from_z, pl.ds(32 * i, 32), :] = part
-        wait_bytes(l3.at[pl.ds(0, 7)], wa_rs)
-        total = jnp.zeros((TOK, 128), F32)
-        for i in range(4):
-            left = jnp.concatenate([lb[2 * i], lb[2 * i + 1]], axis=1)
-            total = total + jnp.dot(left, rb[pl.ds(2 * i, 2)].reshape(256, 128), preferred_element_type=F32)
+            right = jnp.concatenate(turned_parts(yz[from_z].astype(F32)), axis=0)
+            total = total + jnp.dot(lb[from_z], right, preferred_element_type=F32)
         bs[...] = total.reshape(8, 32, 128)
         bs[p] += yz[z].astype(F32)
         ar_s[...] = bs[...].reshape(TOK, 128).astype(BF16)
@@ -209,11 +206,8 @@
     def plane_product(k):
         total = jnp.zeros((TOK, 128), F32)
         for j in range(8):
-            for i, part in enumerate(turned_parts(yb[k, j].astype(F32))):
-                r8[j, pl.ds(32 * i, 32), :] = part
-                r8[j, pl.ds(128 + 32 * i, 32), :] = part
-        for j in range(8):
-            total = total + jnp.dot(lc[j], r8[j], preferred_element_type=F32)
+            parts = turned_parts(yb[k, j].astype(F32))
+            total = total + jnp.dot(lc[j], jnp.concatenate(parts + parts, axis=0), preferred_element_type=F32)
         zs[k] = total.astype(BF16).reshape(8, 32, 128)
         for dz in OFFSETS:
             to_z = lax.rem(z + dz, 8)
@@ -523,6 +517,64 @@
         for j in (2, 3, 1):
             remote(ex.at[slot], ex.at[slot], ex_ss, ex_rs, lax.rem(s + j, 4), z, p).start()
 
+    @pl.when(s < 3)
+    def _():
+        wait_bytes(s0_s, s0_ss)
+
+    @pl.when(s != 2)
+    def _():
+        wait_bytes(ag.at[pl.ds(0, 49)], ap_ss)
+        for i in range(2):
+            wait_bytes(qb.at[pl.ds(0, 28)], qp_ss.at[i])
+
+        @pl.when(z < 7)
+        def _():
+            wait_bytes(ag.at[pl.ds(0, 7)], az_ss)
+
+    @pl.when(s == 1)
+    def _():
+        wait_bytes(qb.at[pl.ds(0, 7)], qz_ss)
+        wait_bytes(q3.at[pl.ds(0, 7)], q3p_ss)
+        wait_bytes(q3.at[pl.ds(0, 56)], q3v_ss)
+
+    @pl.when(s == 3)
+    def _():
+        wait_bytes(qown, qz_ss)
+
+    @pl.when((s == 0) | (s == 2))
+    def _():
+        wait_bytes(qb.at[pl.ds(0, 8)], qz_ss)
+
+    @pl.when((s == 0) | (s == 2))
+    def _():
+        wait_bytes(xr, x_ss)
+
+    @pl.when(s == 3)
+    def _():
+        wait_bytes(sk_s, sk_ss)
+
+    @pl.when((s == 1) | (s == 2))
+    def _():
+        wait_bytes(pb, p_ss)
+        wait_bytes(zs.at[0], z_ss.at[0])
+
+    @pl.when(s >= 2)
+    def _():
+        wait_bytes(l3.at[pl.ds(0, 7)], wa_ss)
+
+    @pl.when(s == 2)
+    def _():
+        wait_bytes(yz.at[pl.ds(0, 7)], v_ss)
+        wait_bytes(ar_r, ar_ss)
+
+    @pl.when(s == 3)
+    def _():
+        for k in range(2):
+            wait_bytes(zs.at[k], z_ss.at[k])
+        wait_bytes(zs.at[2, pl.ds(0, 7)], z_ss.at[2])
+        for k in range(2):
+            wait_bytes(yb.at[k, pl.ds(0, 7)], y_ss.at[k])
+
     @pl.when(s != 2)
     def _():
         wait_bytes(ex.at[pl.ds(0, 2)], ex_rs)
@@ -536,64 +588,9 @@
         mine = mine + jnp.where(s == i, total[:, 32 * i:32 * i + 32], 0.0)
     out_ref[...] = mine[0:2, :]
 
-    @pl.when(s < 3)
-    def _():
-        wait_bytes(s0_s, s0_ss)
-
     @pl.when(s != 2)
     def _():
         wait_bytes(ex, ex_ss)
-        wait_bytes(ag.at[pl.ds(0, 49)], ap_ss)
-        for i in range(2):
-            wait_bytes(qb.at[pl.ds(0, 28)], qp_ss.at[i])
-
-        @pl.when(z < 7)
-        def _():
-            wait_bytes(ag.at[pl.ds(0, 7)], az_ss)
-
-    @pl.when(s == 1)
-    def _():
-        wait_bytes(qb.at[pl.ds(0, 7)], qz_ss)
-        wait_bytes(q3.at[pl.ds(0, 7)], q3p_ss)
-        wait_bytes(q3.at[pl.ds(0, 56)], q3v_ss)
-
-    @pl.when(s == 3)
-    def _():
-        wait_bytes(qown, qz_ss)
-
-    @pl.when((s == 0) | (s == 2))
-    def _():
-        wait_bytes(qb.at[pl.ds(0, 8)], qz_ss)
-
-    @pl.when((s == 0) | (s == 2))
-    def _():
-        wait_bytes(xr, x_ss)
-
-    @pl.when(s == 3)
-    def _():
-        wait_bytes(sk_s, sk_ss)
-
-    @pl.when((s == 1) | (s == 2))
-    def _():
-        wait_bytes(pb, p_ss)
-        wait_bytes(zs.at[0], z_ss.at[0])
-
-    @pl.when(s >= 2)
-    def _():
-        wait_bytes(l3.at[pl.ds(0, 7)], wa_ss)
-
-    @pl.when(s == 2)
-    def _():
-        wait_bytes(yz.at[pl.ds(0, 7)], v_ss)
-        wait_bytes(ar_r, ar_ss)
-
-    @pl.when(s == 3)
-    def _():
-        for k in range(2):
-            wait_bytes(zs.at[k], z_ss.at[k])
-        wait_bytes(zs.at[2, pl.ds(0, 7)], z_ss.at[2])
-        for k in range(2):
-            wait_bytes(yb.at[k, pl.ds(0, 7)], y_ss.at[k])
 
 
 def local(top_grad, activations, weights, proj_in, proj_out, queries, lengths):
@@ -618,8 +615,6 @@
             pltpu.VMEM((8, 256, 128), BF16),
             pltpu.VMEM((8, 256, 256), BF16),
             pltpu.VMEM((256, 128), BF16),
-            pltpu.VMEM((8, 128, 128), BF16),
-            pltpu.VMEM((8, 256, 128), BF16),
             pltpu.VMEM((32, 128), BF16),
             pltpu.VMEM((32, 128), BF16),
             pltpu.VMEM((8, 8, 32, 128), BF16),
@@ -660,7 +655,7 @@
             pltpu.SemaphoreType.REGULAR,
         ],
         compiler_params=pltpu.CompilerParams(
-            collective_id=0, has_side_effects=True, vmem_limit_bytes=64 * 2**20 - 2**17
+            collective_id=0, has_side_effects=True, vmem_limit_bytes=56541184
         ),
         name="chain",
     )(top_grad, activations, weights, proj_in, proj_out, queries, lengths) * 0.125

time: 49.6 us -> 48.7 us (0.982)
  Pallas kernels: 48.2 us -> 47.4 us
  other arithmetic: 1.24 us -> 0.56 us
  local copies, waits for them, and re-layouts: 0 us -> 0.65 us
    pallas_call x1, Pallas kernels: 48.2 us -> 47.4 us  [local(): pl.pallas_call(kernel, out_shape=jax.ShapeDtypeStruct((2, 32), F32), in_s...]
    mul x1, other arithmetic: 1.24 us -> 0.56 us  [local(): pl.pallas_call(kernel, out_shape=jax.ShapeDtypeStruct((2, 32), F32), in_s...]
    unnamed x0 -> x2, local copies, waits for them, and re-layouts: none -> 0.65 us
where the time goes in v6:
time: 48.7 us; the launch traced here: 48.6 us
  Pallas kernels  47.4 us (97%)
  local copies, waits for them, and re-layouts  0.65 us (1%)
  other arithmetic  0.56 us (1%)
    pallas_call x1, Pallas kernels, local(): pl.pallas_call(kernel, out_shape=jax.ShapeDtypeStruct((2, 32), F32), in_s...  47.4 us

profile of v6, /device:TPU:1, one launch (start us, length us, event | category | flops | bytes accessed | tf_op | source)
XLA Modules:
  0.0 48.6 jit_solution(11428693582472926320)
XLA Ops:
  0.0 0.0 copy-start
  0.0 0.7 %copy-done = s32[2]{0:T(128)S(1)} copy-done((s32[2]{0:T(128)S(1)}, s32[2]{0:T(128)}, u32[]{:S(2)}) %copy-start) | copy-done | bytes 32
  0.7 47.4 %chain.1 = f32[2,32]{1,0:T(2,128)S(1)} custom-call(bf16[256,3584]{1,0:T(8,128)(2,1)} %top_ref.1, bf16[1,256,3584]{2,1,0:T(8,128)(2,1)} %act_ref.1, bf16[1,56,3584]{2,1,0:T(8,128)(2,1)} %w_ref.1, bf16[1,64,3584]{2,1,0:T(8,128)(2,1)} %pin_ref.1, bf16[1,64,3584]{2,1,0:T(8,128)(2,1)} %pout_ref.1, bf16[1,2,4096]{2,1,0:T(2,128)(2,1)} %qry_ref.1, s32[2]{0:T(128)S(1)} %copy-done), custom_call_target="tpu_custom_call" | custom-call | tf_op jit(solution)/shard_map/chain/pallas_call | solution.py:599
  48.0 0.6 %broadcast_multiply_fusion = f32[2,32]{1,0:T(2,128)} fusion(f32[2,32]{1,0:T(2,128)S(1)} %chain.1), kind=kLoop, calls=%fused_computation | loop fusion | flops 64 | bytes 512 | tf_op jit(solution)/shard_map/mul | solution.py:599
Async XLA Ops:
  0.0 0.7 %copy-start = (s32[2]{0:T(128)S(1)}, s32[2]{0:T(128)}, u32[]{:S(2)}) copy-start(s32[2]{0:T(128)} %len_ref.1) | copy-start | bytes 28

commit v7 on v6

--- a/solution.py
+++ b/solution.py
@@ -287,8 +287,8 @@
             for dz in OFFSETS[:-1]:
                 remote(ag.at[d], ag.at[d], az_ss, az_rs.at[z], s, lax.rem(z + dz, 8), p).start()
 
-    def gather_plane():
-        for dz in nearest:
+    def gather_plane(distances):
+        for dz in distances:
             from_z = lax.rem(z + dz, 8)
 
             @pl.when(from_z < 7)
@@ -479,12 +479,14 @@
 
     @pl.when(s != 2)
     def _():
-        gather_plane()
+        gather_plane(nearest[:1])
 
         @pl.when(s == 3)
         def _():
             wait_queries(qb, qp_rs.at[1], 28)
             turn_queries(qb, qg, 4, 4)
+
+        gather_plane(nearest[1:])
 
         @pl.when(s == 1)
         def _():

time: 48.7 us -> 49.3 us (1.012)
  Pallas kernels: 47.4 us -> 48 us
    pallas_call x1, Pallas kernels: 47.4 us -> 48 us  [local(): pl.pallas_call(kernel, out_shape=jax.ShapeDtypeStruct((2, 32), F32), in_s...]
where the time goes in v7:
time: 49.3 us; the launch traced here: 49.2 us
  Pallas kernels  48 us (97%)
  local copies, waits for them, and re-layouts  0.65 us (1%)
  other arithmetic  0.56 us (1%)
    pallas_call x1, Pallas kernels, local(): pl.pallas_call(kernel, out_shape=jax.ShapeDtypeStruct((2, 32), F32), in_s...  48 us

profile of v7, /device:TPU:1, one launch (start us, length us, event | category | flops | bytes accessed | tf_op | source)
XLA Modules:
  0.0 49.2 jit_solution(17690354771869530520)
XLA Ops:
  0.0 0.0 copy-start
  0.0 0.7 %copy-done = s32[2]{0:T(128)S(1)} copy-done((s32[2]{0:T(128)S(1)}, s32[2]{0:T(128)}, u32[]{:S(2)}) %copy-start) | copy-done | bytes 32
  0.7 48.0 %chain.1 = f32[2,32]{1,0:T(2,128)S(1)} custom-call(bf16[256,3584]{1,0:T(8,128)(2,1)} %top_ref.1, bf16[1,256,3584]{2,1,0:T(8,128)(2,1)} %act_ref.1, bf16[1,56,3584]{2,1,0:T(8,128)(2,1)} %w_ref.1, bf16[1,64,3584]{2,1,0:T(8,128)(2,1)} %pin_ref.1, bf16[1,64,3584]{2,1,0:T(8,128)(2,1)} %pout_ref.1, bf16[1,2,4096]{2,1,0:T(2,128)(2,1)} %qry_ref.1, s32[2]{0:T(128)S(1)} %copy-done), custom_call_target="tpu_custom_call" | custom-call | tf_op jit(solution)/shard_map/chain/pallas_call | solution.py:601
  48.6 0.6 %broadcast_multiply_fusion = f32[2,32]{1,0:T(2,128)} fusion(f32[2,32]{1,0:T(2,128)S(1)} %chain.1), kind=kLoop, calls=%fused_computation | loop fusion | flops 64 | bytes 512 | tf_op jit(solution)/shard_map/mul | solution.py:601
Async XLA Ops:
  0.0 0.7 %copy-start = (s32[2]{0:T(128)S(1)}, s32[2]{0:T(128)}, u32[]{:S(2)}) copy-start(s32[2]{0:T(128)} %len_ref.1) | copy-start | bytes 28
